TPU v7x, 32 devices: a whole 2x2x4 slice. The times are simulated.
32 devices in a mesh: grp: 2 (over x), facet: 16 (over z, y, core).
Axes of the slice: x: 2, y: 2, z: 4, core: 2. Of those that a mesh axis runs over, the one named last changes fastest.
Arguments:
- subgrids: bfloat16 [32, 2, 8192, 128], P(('grp', 'facet')), parts along dimension 0, may hold values from -6 to 6
- taper: float32 [8192], replicated, may hold values from 0.1 to 1.9
- counts: int32 [32], P(('grp', 'facet')), parts along dimension 0, may hold values from 0 to 199, as said below
- positions: int32 [32], P(('grp', 'facet')), parts along dimension 0, may hold values from 0 to 7
- channels: int32 [32], P(('grp', 'facet')), parts along dimension 0, may hold values from 0 to 95
- correction: float32 [65536], P('facet'), may hold values from 0.5 to 1.5
Outputs:
- image: float32 [2, 2, 65536, 256], P(None, None, 'facet', 'grp'), parts along dimension 3
There are 2 independent parts, one for each index of `grp`. A program takes and returns all parts, laid end to end along the dimension named above; an argument that names none is the same for every part. Nothing has to cross between parts.
Inputs may be any that keep to these rules, and one draw needn't show every extreme that they name: `counts`: 0 means an empty subgrid; the share of empty subgrids differs from device to device; in each part at least one subgrid is non-empty.
All inputs are finite; a program needn't handle non-finite values.
Results may differ from a plain program's by a relative error of at most 0.0029.
Values may be sent and summed in bfloat16 or wider, within the bound.
No kernel may reach another device: no remote copies, remote signals or barrier semaphores. Data moves between devices by JAX's collectives and lax.ppermute only.
A program may use at most 128 MiB of HBM per device.

v0:
```python
import functools
import math

import jax
import jax.numpy as jnp
import numpy as np
from jax import lax
from jax.experimental import pallas as pl
from jax.experimental.pallas import tpu as pltpu
from jax.sharding import PartitionSpec as P

TAYLOR = 2
CHANNELS = 96
MIB = 1024 * 1024
f32 = jnp.float32
bf16 = jnp.bfloat16

PITCH, PITCH_MID, PITCH_STAGE, PITCH_IMAGE = 136, 264, 72, 72


def split(value):
    high = value.astype(bf16)
    return high, (value - high.astype(f32)).astype(bf16)


def forward_tables():
    b = np.arange(128)[:, None, None]
    ka = np.arange(64)[None, :, None]
    a = np.arange(64)[None, None, :]
    angle = 2 * np.pi * (((128 * a + b) * ka) % 8192) / 8192.0
    first = np.concatenate([np.cos(angle), np.sin(angle)], axis=2).astype(np.float32)
    kb = np.arange(128)[:, None]
    angle = 2 * np.pi * ((kb * kb.T) % 128) / 128
    cos = (np.cos(angle) / math.sqrt(8192.0)).reshape(16, 8, 128)
    sin = (np.sin(angle) / math.sqrt(8192.0)).reshape(16, 8, 128)
    second = np.empty((16, 8, 2, 2, 128))
    second[:, :, 0, 0], second[:, :, 0, 1] = cos, sin
    second[:, :, 1, 0], second[:, :, 1, 1] = -sin, cos
    second = second.reshape(256, 256).astype(np.float32)
    high = second.astype(bf16)
    low = (second - high.astype(np.float32)).astype(bf16)
    return first, np.concatenate([high, low], axis=1)


def inverse_table():
    k1 = np.arange(64)[:, None, None]
    k2 = np.arange(64)[None, :, None]
    cell = np.arange(64)[None, None, :]
    angle = 2 * np.pi * ((cell * (k1 + 64 * k2)) % 4096) / 4096.0
    cos, sin = np.cos(angle) / 64.0, np.sin(angle) / 64.0
    table = np.empty((64, 2, 64, 2, 64), np.float32)
    table[:, 0, :, 0], table[:, 0, :, 1] = cos, -sin
    table[:, 1, :, 0], table[:, 1, :, 1] = sin, cos
    return table.reshape(64, 128, 128)


def forward_kernel(*rest, subset, starts, count, extra):
    if extra:
        meta_ref, *rest = rest
    sub_hbm, taper_ref, first_hbm, second_ref, *rest = rest
    outs = rest[: len(subset)]
    sub_ref, first_ref, plain, tapers, mid, pieces, sub_sem, first_sem, out_sem = rest[len(subset) :]
    sub_copies, first_copies, out_copies = [], [], []
    for q in range(4):
        for x in range(2):
            rows = pl.ds(q * 2048, 2048)
            copy = pltpu.make_async_copy(sub_hbm.at[x, rows], sub_ref.at[x, rows], sub_sem.at[q, x])
            copy.start()
            sub_copies.append(copy)
    for q in range(4):
        rows = pl.ds(q * 32, 32)
        copy = pltpu.make_async_copy(first_hbm.at[rows], first_ref.at[rows], first_sem.at[q])
        copy.start()
        first_copies.append(copy)
    turned = taper_ref[...].T
    tapers[:, 0:64] = turned
    tapers[:, 64:128] = turned
    for q in range(4):
        sub_copies[2 * q].wait()
        sub_copies[2 * q + 1].wait()

        @pl.loop(16 * q, 16 * q + 16, unroll=4)
        def _(a):
            rows = pl.ds(pl.multiple_of(a * 128, 128), 128)
            plain[pl.ds(pl.multiple_of(a * PITCH, 8), 128), :] = sub_ref[0, rows, :].astype(f32)
            plain[pl.ds(pl.multiple_of((64 + a) * PITCH, 8), 128), :] = sub_ref[1, rows, :].astype(f32)

    lane = lax.broadcasted_iota(jnp.int32, (1, 128), 1)
    sign = jnp.where(lane < 64, -1.0, 1.0).astype(f32)

    def operands(b):
        data = plain[pl.ds(b, 128, stride=PITCH), :].astype(bf16)
        taper = tapers[pl.ds(b, 1), :]
        table = first_ref[b]
        real = table * taper
        imag = pltpu.roll(table, 64, 1) * (taper * sign)
        high, low = split(jnp.concatenate([real, imag], axis=0))
        return data, jnp.concatenate([high, low], axis=1)

    for q in range(4):
        first_copies[q].wait()

        @pl.loop(16 * q, 16 * q + 16, unroll=16)
        def _(pair):
            data_a, matrix_a = operands(2 * pair)
            data_b, matrix_b = operands(2 * pair + 1)
            data = jnp.concatenate([data_a, data_b], axis=1)
            out = jnp.dot(
                jnp.concatenate([matrix_a, matrix_b], axis=0),
                jnp.concatenate([data, data], axis=0),
                preferred_element_type=f32,
            )
            for j in range(2):
                b = 2 * pair + j
                mine = out[2 * count * j : 2 * count * (j + 1), 128 * j : 128 * j + 128]
                mid[pl.ds(b, count, stride=PITCH_MID), :] = mine[:count]
                mid[pl.ds(128 + b, count, stride=PITCH_MID), :] = mine[count:]

    me = lax.axis_index("facet")
    blocks = [pl.ds(pl.multiple_of((me ^ s) * 16, 16), 16) for s in subset]
    high = jnp.concatenate([second_ref[rows, 0:256] for rows in blocks], axis=0)
    low = jnp.concatenate([second_ref[rows, 256:512] for rows in blocks], axis=0)
    rows = 16 * len(subset)
    if extra:
        row = lax.broadcasted_iota(jnp.int32, (16, 128), 0)
        tile = jnp.where(row == 0, meta_ref[0], jnp.where(row == 1, meta_ref[1], meta_ref[2]))
        tile = tile.astype(f32).astype(bf16)
        for i in range(len(subset)):
            pieces[i, count] = tile
    part = count // 2
    for half in range(2):

        @pl.loop(part // 2 * half, part // 2 * (half + 1), unroll=8)
        def _(pair):
            both = []
            for j in range(2):
                start = pl.multiple_of((2 * pair + j) * PITCH_MID, 8)
                both.append(mid[pl.ds(start, 256), :])
            data_high, data_low = split(jnp.concatenate(both, axis=1))
            out = jnp.dot(jnp.concatenate([high, low], axis=0), data_high, preferred_element_type=f32)
            out = out[:rows] + out[rows:] + jnp.dot(high, data_low, preferred_element_type=f32)
            out = out.astype(bf16)
            for i in range(len(subset)):
                for j in range(2):
                    pieces[i, 2 * pair + j] = out[i * 16 : i * 16 + 16, j * 128 : j * 128 + 128]

        size = part + (extra if half else 0)
        for i, start in enumerate(starts):
            if half * part >= start:
                copy = pltpu.make_async_copy(
                    pieces.at[i, pl.ds(half * part, size)],
                    outs[i].at[pl.ds(half * part - start, size)],
                    out_sem.at[half, i],
                )
                copy.start()
                out_copies.append(copy)
    for copy in out_copies:
        copy.wait()


def forward(subgrid, taper, first, second, subset, starts, meta=None):
    number, count, extra = len(subset), first.shape[1], 0 if meta is None else 1
    shapes = [jax.ShapeDtypeStruct((count - start + extra, 16, 128), bf16) for start in starts]
    hbm = pl.BlockSpec(memory_space=pl.ANY)
    return pl.pallas_call(
        functools.partial(forward_kernel, subset=subset, starts=starts, count=count, extra=extra),
        grid=(1,),
        in_specs=[pl.BlockSpec(memory_space=pltpu.SMEM)] * extra
        + [
            hbm,
            pl.BlockSpec((64, 128), lambda i: (0, 0)),
            hbm,
            pl.BlockSpec((256, 512), lambda i: (0, 0)),
        ],
        out_specs=[hbm] * number,
        out_shape=shapes,
        scratch_shapes=[
            pltpu.VMEM((2, 8192, 128), bf16),
            pltpu.VMEM((128, count, 128), f32),
            pltpu.VMEM((128 * PITCH, 128), f32),
            pltpu.VMEM((128, 128), f32),
            pltpu.VMEM((count * PITCH_MID, 128), f32),
            pltpu.VMEM((number, count + extra, 16, 128), bf16),
            pltpu.SemaphoreType.DMA((4, 2)),
            pltpu.SemaphoreType.DMA((4,)),
            pltpu.SemaphoreType.DMA((2, number)),
        ],
        compiler_params=pltpu.CompilerParams(vmem_limit_bytes=58 * MIB),
        cost_estimate=pl.CostEstimate(flops=160000000 * count, bytes_accessed=12 * MIB, transcendentals=0),
        name=f"forward{number}",
    )(*([meta] * extra), subgrid, taper, first, second)


def placing_matrix(tiles):
    owner = lax.broadcasted_iota(jnp.int32, (16, 256), 1) >> 4
    meta = jnp.zeros((16, 256), f32)
    for s, tile in enumerate(tiles):
        tile = tile.astype(f32)
        meta = jnp.where(owner == s, jnp.concatenate([tile, tile], axis=1), meta)
    counts, positions, channels = meta[0:1], meta[1:2].astype(jnp.int32), meta[2:3]
    root = jnp.sqrt(counts)
    weight = root * (16.0 / (jnp.sum(root, axis=1, keepdims=True) * (1.0 / 16)))
    half = 0.5 * (CHANNELS - 1)
    level = (channels - half) / half
    row = lax.broadcasted_iota(jnp.int32, (128, 256), 0)
    lane = lax.broadcasted_iota(jnp.int32, (128, 256), 1)
    n1 = positions * 8 + ((lane >> 1) & 7)
    index = (n1 * (row >> 1) + 16 * ((lane & 1) - (row & 1))) & 63
    wave = jnp.cos(index.astype(f32) * (2 * math.pi / 64))
    return jnp.concatenate([wave * weight, wave * (weight * level)], axis=0)


def scale_kernel(correction_ref, table_ref, scaled_ref):
    gains = correction_ref[...].T
    gains = jnp.concatenate([gains, gains], axis=1).T
    for k1 in range(64):
        high, low = split(table_ref[k1] * gains[:, k1 : k1 + 1])
        scaled_ref[k1, :, 0:128] = high
        scaled_ref[k1, :, 128:256] = low


def scale(correction, table):
    whole = lambda shape: pl.BlockSpec(shape, lambda i: (0,) * len(shape))
    shape = jax.ShapeDtypeStruct((64, 128, 256), bf16)
    return pl.pallas_call(
        scale_kernel,
        grid=(1,),
        in_specs=[whole(correction.shape), whole(table.shape)],
        out_specs=whole(shape.shape),
        out_shape=shape,
        compiler_params=pltpu.CompilerParams(vmem_limit_bytes=58 * MIB, dimension_semantics=("arbitrary",)),
        cost_estimate=pl.CostEstimate(flops=6000000000, bytes_accessed=16 * MIB, transcendentals=0),
        name="scale",
    )(correction, table)


def final_kernel(scaled_hbm, *rest, sizes):
    refs = rest[: len(sizes)]
    out_hbm, store, held, scaled_ref, image, piece_sem, scaled_sem, out_sem = rest[len(sizes) :]
    scaled_copies, out_copies = [], []
    piece_copies = [[], [], []]

    def fetch(ref, at, s, stage, start, size):
        target = held.at[s, pl.ds(start, size)]
        copy = pltpu.make_async_copy(ref.at[pl.ds(at, size)], target, piece_sem.at[stage, s])
        copy.start()
        piece_copies[stage].append(copy)

    wholes = refs[len(sizes) - 16 :]
    halves = refs[: len(sizes) - 16]
    for s, ref in enumerate(wholes):
        fetch(ref, ref.shape[0] - 1, s, 0, 64, 1)
    for s, ref in enumerate(wholes):
        fetch(halves[s] if s < len(halves) else ref, 0, s, 1, 0, 32)
    for s, ref in enumerate(wholes):
        fetch(ref, 0 if s < len(halves) else 32, s, 2, 32, 32)
    for q in range(4):
        part = pl.ds(16 * q, 16)
        copy = pltpu.make_async_copy(scaled_hbm.at[part], scaled_ref.at[part], scaled_sem.at[q])
        copy.start()
        scaled_copies.append(copy)
    for copy in piece_copies[0]:
        copy.wait()
    high, low = split(placing_matrix([held[s, 64] for s in range(16)]))
    for half in range(2):
        for copy in piece_copies[1 + half]:
            copy.wait()

        @pl.loop(16 * half, 16 * half + 16, unroll=8)
        def _(pair):
            both = [jnp.concatenate([held[s, 2 * pair + j] for s in range(16)], axis=0) for j in range(2)]
            data = jnp.concatenate(both, axis=1)
            out = jnp.dot(high, data, preferred_element_type=f32) + jnp.dot(low, data, preferred_element_type=f32)
            for j in range(2):
                store[pl.ds(2 * pair + j, 256, stride=PITCH_STAGE), :] = out[:, j * 128 : j * 128 + 128]

    for copy in scaled_copies:
        copy.wait()
    for t in range(2):

        @pl.loop(0, 64, unroll=32)
        def _(k1):
            row = (t * 64 + k1) * (2 * PITCH_STAGE)
            parts = [store[pl.ds(pl.multiple_of(row + x * PITCH_STAGE, 8), 64), :] for x in range(2)]
            data = jnp.concatenate(parts, axis=0).astype(bf16)
            out = jnp.dot(scaled_ref[k1], jnp.concatenate([data, data], axis=0), preferred_element_type=f32)
            for x in range(2):
                start = (t * 2 + x) * (64 * PITCH_IMAGE)
                image[pl.ds(start + k1, 64, stride=PITCH_IMAGE), :] = out[x * 64 : x * 64 + 64]

        for x in range(2):
            source = image.reshape(4, 64, PITCH_IMAGE, 128).at[t * 2 + x, :, pl.ds(0, 64)]
            copy = pltpu.make_async_copy(source, out_hbm.at[t, x], out_sem.at[t, x])
            copy.start()
            out_copies.append(copy)
    for copy in out_copies:
        copy.wait()


def final(scaled, pieces):
    hbm = pl.BlockSpec(memory_space=pl.ANY)
    sizes = tuple(piece.shape[0] for piece in pieces)
    return pl.pallas_call(
        functools.partial(final_kernel, sizes=sizes),
        in_specs=[hbm] * (1 + len(pieces)),
        out_specs=hbm,
        out_shape=jax.ShapeDtypeStruct((2, 2, 64, 64, 128), f32),
        scratch_shapes=[
            pltpu.VMEM((256 * PITCH_STAGE, 128), f32),
            pltpu.VMEM((16, 65, 16, 128), bf16),
            pltpu.VMEM((64, 128, 256), bf16),
            pltpu.VMEM((4 * 64 * PITCH_IMAGE, 128), f32),
            pltpu.SemaphoreType.DMA((3, 16)),
            pltpu.SemaphoreType.DMA((4,)),
            pltpu.SemaphoreType.DMA((2, 2)),
        ],
        compiler_params=pltpu.CompilerParams(vmem_limit_bytes=58 * MIB),
        cost_estimate=pl.CostEstimate(flops=8000000000, bytes_accessed=16 * MIB, transcendentals=0),
        name="final",
    )(scaled, *pieces)


EARLY = (8, 9, 10)
LATE = (8, 9, 10, 3, 11, 2, 12, 1, 4, 13, 5, 6, 14, 7, 15)


def exchange(piece, s):
    return lax.ppermute(piece, "facet", [(i, i ^ s) for i in range(16)])


def local(subgrids, taper, counts, positions, channels, correction):
    first, second = forward_tables()
    inputs = (subgrids[0], taper.reshape(64, 128))
    early = forward(*inputs, first[:, :32], second, EARLY, (0,) * len(EARLY))
    starts = tuple(32 if s in EARLY else 0 for s in LATE) + (0,)
    meta = jnp.concatenate([counts, positions, channels])
    late = forward(*inputs, first, second, LATE + (0,), starts, meta)
    early = [exchange(piece, s) for s, piece in zip(EARLY, early)]
    late = [exchange(piece, s) for s, piece in zip(LATE, late)] + [late[15]]
    scaled = scale(correction.reshape(64, 64), inverse_table())
    image = final(scaled, early + late)
    return image.reshape(TAYLOR, 2, 4096, 128)


def phase_table(height, breadth, length, sign):
    first = jnp.arange(height, dtype=jnp.int32)[:, None]
    second = jnp.arange(breadth, dtype=jnp.int32)[None, :]
    angle = (first * second % length).astype(jnp.float32) * (2.0 * math.pi / length)
    return (jnp.cos(angle), sign * jnp.sin(angle))


def transform(real_part, imag_part, sign):
    length = real_part.shape[-2]
    width = real_part.shape[-1]
    outer = math.gcd(length, 64)
    inner = length // outer
    leading = real_part.shape[:-2]
    real_in = real_part.reshape(leading + (outer, inner, width))
    imag_in = imag_part.reshape(leading + (outer, inner, width))
    high = lax.Precision.HIGHEST
    outer_re, outer_im = phase_table(outer, outer, outer, sign)
    twist_re, twist_im = phase_table(outer, inner, length, sign)
    twist_re = twist_re[:, :, None]
    twist_im = twist_im[:, :, None]
    inner_re, inner_im = phase_table(inner, inner, inner, sign)
    first_re = jnp.einsum("ka,...abr->...kbr", outer_re, real_in, precision=high) - jnp.einsum(
        "ka,...abr->...kbr", outer_im, imag_in, precision=high
    )
    first_im = jnp.einsum("ka,...abr->...kbr", outer_re, imag_in, precision=high) + jnp.einsum(
        "ka,...abr->...kbr", outer_im, real_in, precision=high
    )
    turned_re = first_re * twist_re - first_im * twist_im
    turned_im = first_re * twist_im + first_im * twist_re
    last_re = jnp.einsum("bm,...kbr->...mkr", inner_re, turned_re, precision=high) - jnp.einsum(
        "bm,...kbr->...mkr", inner_im, turned_im, precision=high
    )
    last_im = jnp.einsum("bm,...kbr->...mkr", inner_im, turned_re, precision=high) + jnp.einsum(
        "bm,...kbr->...mkr", inner_re, turned_im, precision=high
    )
    factor = 1.0 / math.sqrt(length)
    return (
        last_re.reshape(leading + (length, width)) * factor,
        last_im.reshape(leading + (length, width)) * factor,
    )


def general(subgrids, taper, counts, positions, channels, correction):
    local_count = subgrids.shape[0]
    facets = lax.axis_size("facet")
    every_count, every_position, every_channel = (
        lax.all_gather(counts, "facet", axis=0, tiled=True),
        lax.all_gather(positions, "facet", axis=0, tiled=True),
        lax.all_gather(channels, "facet", axis=0, tiled=True),
    )
    data = subgrids[0].astype(jnp.float32) * taper[:, None]
    wave_re, wave_im = transform(data[0], data[1], -1.0)
    block = jnp.stack([wave_re, wave_im]).astype(jnp.bfloat16)[None]
    received_list = [lax.all_to_all(block, "facet", split_axis=2, concat_axis=0, tiled=True)]
    stacked = jnp.stack(received_list, axis=1)
    received = stacked.reshape((facets * local_count,) + stacked.shape[2:])
    root = jnp.sqrt(every_count.astype(jnp.float32))
    weight = root * (root.shape[0] / jnp.sum(root))
    half = 0.5 * (CHANNELS - 1)
    level = (every_channel.astype(jnp.float32) - half) / half
    terms = [weight]
    terms.append(terms[-1] * level)
    taylor = jnp.stack(terms)
    contrib = received.shape[2]
    rows = received.shape[3]
    slot_count = correction.shape[0] // contrib
    slots = (every_position[None, :] == jnp.arange(slot_count, dtype=jnp.int32)[:, None]).astype(
        jnp.float32
    )
    table = taylor[:, None, :] * slots[None]
    buffer = jnp.einsum(
        "tqs,sxcr->txqcr", table, received.astype(jnp.float32), precision=lax.Precision.HIGHEST
    )
    buffer = buffer.reshape(TAYLOR, 2, slot_count * contrib, rows)
    field_re, field_im = transform(buffer[:, 0], buffer[:, 1], 1.0)
    return jnp.stack([field_re, field_im], axis=1) * correction[:, None]


def solution(mesh):
    placed = (
        P(("grp", "facet"), None, None, None),
        P(),
        P(("grp", "facet")),
        P(("grp", "facet")),
        P(("grp", "facet")),
        P("facet"),
    )
    own = local if mesh.shape["facet"] == 16 else general
    return jax.shard_map(
        own, mesh=mesh, in_specs=placed, out_specs=P(None, None, "facet", "grp"), check_vma=False
    )
```

profile of v0, /device:TPU:1, one launch (start us, length us, event | category | flops | bytes accessed | tf_op | source)
XLA Modules:
  0.0 131.1 jit_solution(1938802344427030507)
XLA Ops:
  0.0 8.3 %forward3.1 = (bf16[32,16,128]{2,1,0:T(8,128)(2,1)}, bf16[32,16,128]{2,1,0:T(8,128)(2,1)}, bf16[32,16,128]{2,1,0:T(8,128)(2,1)}) custom-call(bf16[2,8192,128]{2,1,0:T(8,128)(2,1)} %bitcast.3, f32[64,128]{1,0:T(8,128)} %bitcast.5, f32[128,32,128]{2,1,0:T(8,128)} %constant.8.clone.rest_2_, bf16[256,512]{1,0:T(8,128)(2,1)} %constant.9.clone.rest_3_.rest_4_), custom_call_target="tpu_custom_call" | custom-call | flops 5120000000 | bytes 12582912 | tf_op jit(solution)/shard_map/forward3/pallas_call | solution.py:165
  8.3 3.2 %collective-permute-start = (bf16[32,16,128]{2,1,0:T(8,128)(2,1)}, bf16[32,16,128]{2,1,0:T(8,128)(2,1)S(1)}, u32[]{:S(2)}, u32[]{:S(2)}) collective-permute-start(bf16[32,16,128]{2,1,0:T(8,128)(2,1)} %get-tuple-element.24), channel_id=1, source_target_pairs={{0,8},{1,9},{2,10},{3,11},{4,12},{5,13},{6,14},{7,15},{8,0},{9,1},... | collective-permute-start | bytes 393224 | tf_op jit(solution)/shard_map/ppermute | solution.py:328
  11.5 0.6 collective-permute-start.1
  12.1 3.5 %collective-permute-start.2 = (bf16[32,16,128]{2,1,0:T(8,128)(2,1)}, bf16[32,16,128]{2,1,0:T(8,128)(2,1)S(1)}, u32[]{:S(2)}, u32[]{:S(2)}) collective-permute-start(bf16[32,16,128]{2,1,0:T(8,128)(2,1)} %get-tuple-element.26), channel_id=1, source_target_pairs={{0,10},{1,11},{2,8},{3,9},{4,14},{5,15},{6,12},{7,13},{8,2},{9,3},... | collective-permute-start | bytes 393224 | tf_op jit(solution)/shard_map/ppermute | solution.py:328
  17.6 0.6 pad_add_fusion.rest_0_
  18.2 14.2 %forward16.1 = (bf16[33,16,128]{2,1,0:T(8,128)(2,1)}, bf16[33,16,128]{2,1,0:T(8,128)(2,1)}, bf16[33,16,128]{2,1,0:T(8,128)(2,1)}, bf16[65,16,128]{2,1,0:T(8,128)...) custom-call(s32[3]{0:T(128)} %pad_add_fusion.rest_0_, ...), custom_call_target="tpu_custom_call" | custom-call | flops 10240000000 | bytes 12582912 | tf_op jit(solution)/shard_map/forward16/pallas_call | solution.py:165
  32.4 0.1 collective-permute-start.6
  32.4 1.5 %collective-permute-start.7 = (bf16[65,16,128]{2,1,0:T(8,128)(2,1)}, bf16[65,16,128]{2,1,0:T(8,128)(2,1)S(1)}, u32[]{:S(2)}, u32[]{:S(2)}) collective-permute-start(bf16[65,16,128]{2,1,0:T(8,128)(2,1)} %get-tuple-element.31), channel_id=1, source_target_pairs={{0,11},{1,10},{2,9},{3,8},{4,15},{5,14},{6,13},{7,12},{8,3},{9,2},... | collective-permute-start | bytes 798728 | tf_op jit(solution)/shard_map/ppermute | solution.py:328
  34.0 0.0 collective-permute-done.rest_0_
  34.0 2.3 %collective-permute-start.3 = (bf16[33,16,128]{2,1,0:T(8,128)(2,1)}, bf16[33,16,128]{2,1,0:T(8,128)(2,1)S(1)}, u32[]{:S(2)}, u32[]{:S(2)}) collective-permute-start(bf16[33,16,128]{2,1,0:T(8,128)(2,1)} %get-tuple-element.27), channel_id=1, source_target_pairs={{0,8},{1,9},{2,10},{3,11},{4,12},{5,13},{6,14},{7,15},{8,0},{9,1},... | collective-permute-start | bytes 405512 | tf_op jit(solution)/shard_map/ppermute | solution.py:328
  36.3 0.0 collective-permute-done.1.rest_1_
  36.3 0.6 collective-permute-start.4
  36.8 0.0 collective-permute-done.2.rest_2_
  36.8 1.9 %collective-permute-start.5 = (bf16[33,16,128]{2,1,0:T(8,128)(2,1)}, bf16[33,16,128]{2,1,0:T(8,128)(2,1)S(1)}, u32[]{:S(2)}, u32[]{:S(2)}) collective-permute-start(bf16[33,16,128]{2,1,0:T(8,128)(2,1)} %get-tuple-element.29), channel_id=1, source_target_pairs={{0,10},{1,11},{2,8},{3,9},{4,14},{5,15},{6,12},{7,13},{8,2},{9,3},... | collective-permute-start | bytes 405512 | tf_op jit(solution)/shard_map/ppermute | solution.py:328
  38.7 22.0 %collective-permute-done.3.rest_3_ = bf16[33,16,128]{2,1,0:T(8,128)(2,1)S(1)} collective-permute-done((bf16[33,16,128]{2,1,0:T(8,128)(2,1)}, bf16[33,16,128]{2,1,0:T(8,128)(2,1)S(1)}, u32[]{:S(2)}, u32[]{:S(2)}) %collective-permute-start.3) | collective-permute-done | bytes 135200 | tf_op jit(solution)/shard_map/ppermute | solution.py:328
  60.7 0.1 collective-permute-start.8
  60.8 2.8 %collective-permute-done.4.rest_4_ = bf16[33,16,128]{2,1,0:T(8,128)(2,1)S(1)} collective-permute-done((bf16[33,16,128]{2,1,0:T(8,128)(2,1)}, bf16[33,16,128]{2,1,0:T(8,128)(2,1)S(1)}, u32[]{:S(2)}, u32[]{:S(2)}) %collective-permute-start.4) | collective-permute-done | bytes 135200 | tf_op jit(solution)/shard_map/ppermute | solution.py:328
  63.6 1.0 collective-permute-start.9
  64.6 1.7 %collective-permute-done.5.rest_5_ = bf16[33,16,128]{2,1,0:T(8,128)(2,1)S(1)} collective-permute-done((bf16[33,16,128]{2,1,0:T(8,128)(2,1)}, bf16[33,16,128]{2,1,0:T(8,128)(2,1)S(1)}, u32[]{:S(2)}, u32[]{:S(2)}) %collective-permute-start.5) | collective-permute-done | bytes 135200 | tf_op jit(solution)/shard_map/ppermute | solution.py:328
  66.3 0.7 collective-permute-start.10
  67.0 0.0 collective-permute-done.6.rest_6_
  67.0 0.0 collective-permute-start.11
  67.0 0.0 collective-permute-done.7.rest_7_
  67.0 0.0 copy-start.2
  67.0 1.0 collective-permute-start.12
  68.0 0.0 copy-done
  68.0 0.7 reshape.9.correction_ref
  68.7 3.3 %collective-permute-done.8.rest_8_ = bf16[65,16,128]{2,1,0:T(8,128)(2,1)S(1)} collective-permute-done((bf16[65,16,128]{2,1,0:T(8,128)(2,1)}, bf16[65,16,128]{2,1,0:T(8,128)(2,1)S(1)}, u32[]{:S(2)}, u32[]{:S(2)}) %collective-permute-start.8) | collective-permute-done | bytes 266272 | tf_op jit(solution)/shard_map/ppermute | solution.py:328
  72.0 0.0 collective-permute-start.13
  72.0 1.3 collective-permute-done.9.rest_9_
  73.3 4.7 %collective-permute-start.14 = (bf16[65,16,128]{2,1,0:T(8,128)(2,1)}, bf16[65,16,128]{2,1,0:T(8,128)(2,1)S(1)}, u32[]{:S(2)}, u32[]{:S(2)}) collective-permute-start(bf16[65,16,128]{2,1,0:T(8,128)(2,1)} %get-tuple-element.38), channel_id=1, source_target_pairs={{0,6},{1,7},{2,4},{3,5},{4,2},{5,3},{6,0},{7,1},{8,14},{9,15},{10,... | collective-permute-start | bytes 798728 | tf_op jit(solution)/shard_map/ppermute | solution.py:328
  78.0 0.0 collective-permute-done.10.rest_10_
  78.0 1.8 %collective-permute-start.15 = (bf16[65,16,128]{2,1,0:T(8,128)(2,1)}, bf16[65,16,128]{2,1,0:T(8,128)(2,1)S(1)}, u32[]{:S(2)}, u32[]{:S(2)}) collective-permute-start(bf16[65,16,128]{2,1,0:T(8,128)(2,1)} %get-tuple-element.39), channel_id=1, source_target_pairs={{0,14},{1,15},{2,12},{3,13},{4,10},{5,11},{6,8},{7,9},{8,6},{9,7},... | collective-permute-start | bytes 798728 | tf_op jit(solution)/shard_map/ppermute | solution.py:328
  79.8 0.8 collective-permute-done.11.rest_11_
  80.6 0.0 collective-permute-start.16
  80.6 5.5 %collective-permute-done.12.rest_12_ = bf16[65,16,128]{2,1,0:T(8,128)(2,1)S(1)} collective-permute-done((bf16[65,16,128]{2,1,0:T(8,128)(2,1)}, bf16[65,16,128]{2,1,0:T(8,128)(2,1)S(1)}, u32[]{:S(2)}, u32[]{:S(2)}) %collective-permute-start.12) | collective-permute-done | bytes 266272 | tf_op jit(solution)/shard_map/ppermute | solution.py:328
  86.1 0.0 collective-permute-start.17
  86.1 5.8 %scale.1.scaled_hbm = bf16[64,128,256]{2,1,0:T(8,128)(2,1)} custom-call(f32[64,64]{1,0:T(8,128)} %reshape.9.correction_ref, f32[64,128,128]{2,1,0:T(8,128)} %constant.11.clone.table_ref), custom_call_target="tpu_custom_call" | custom-call | flops 6000000000 | bytes 16777216 | tf_op jit(solution)/shard_map/scale/pallas_call | solution.py:225
  91.9 0.0 copy-done.16
  92.0 0.0 collective-permute-done.13.rest_13_
  92.0 0.0 copy-start.8
  92.0 5.0 %collective-permute-done.14.rest_14_ = bf16[65,16,128]{2,1,0:T(8,128)(2,1)S(1)} collective-permute-done((bf16[65,16,128]{2,1,0:T(8,128)(2,1)}, bf16[65,16,128]{2,1,0:T(8,128)(2,1)S(1)}, u32[]{:S(2)}, u32[]{:S(2)}) %collective-permute-start.14) | collective-permute-done | bytes 266272 | tf_op jit(solution)/shard_map/ppermute | solution.py:328
  97.1 8.2 %collective-permute-done.15.rest_15_ = bf16[65,16,128]{2,1,0:T(8,128)(2,1)S(1)} collective-permute-done((bf16[65,16,128]{2,1,0:T(8,128)(2,1)}, bf16[65,16,128]{2,1,0:T(8,128)(2,1)S(1)}, u32[]{:S(2)}, u32[]{:S(2)}) %collective-permute-start.15) | collective-permute-done | bytes 266272 | tf_op jit(solution)/shard_map/ppermute | solution.py:328
  105.3 6.3 %collective-permute-done.16.rest_16_ = bf16[65,16,128]{2,1,0:T(8,128)(2,1)S(1)} collective-permute-done((bf16[65,16,128]{2,1,0:T(8,128)(2,1)}, bf16[65,16,128]{2,1,0:T(8,128)(2,1)S(1)}, u32[]{:S(2)}, u32[]{:S(2)}) %collective-permute-start.16) | collective-permute-done | bytes 266272 | tf_op jit(solution)/shard_map/ppermute | solution.py:328
  111.6 8.8 %collective-permute-done.17.rest_17_ = bf16[65,16,128]{2,1,0:T(8,128)(2,1)S(1)} collective-permute-done((bf16[65,16,128]{2,1,0:T(8,128)(2,1)}, bf16[65,16,128]{2,1,0:T(8,128)(2,1)S(1)}, u32[]{:S(2)}, u32[]{:S(2)}) %collective-permute-start.17) | collective-permute-done | bytes 266272 | tf_op jit(solution)/shard_map/ppermute | solution.py:328
  120.3 0.0 copy-done.10
  120.3 0.7 copy-done.12
  121.0 9.9 %final.1 = f32[2,2,64,64,128]{4,3,2,1,0:T(8,128)} custom-call(bf16[64,128,256]{2,1,0:T(8,128)(2,1)} %scale.1.scaled_hbm, bf16[32,16,128]{2,1,0:T(8,128)(2,1)} %copy-done.16, bf16[32,16,128]{2,1,0:T(8,128)(2,1)} %copy-done.17, bf16[32,16,128]{2,1,0:T(8,128)(2,1)} %copy-done.18, bf16[33,16,128]{2,1,0:T(8,128)(2,1)} %copy-done.13, ...), custom_call_target="tpu_custom_call" | custom-call | flops 8000000000 | bytes 16777216 | tf_op jit(solution)/shard_map/final/pallas_call | solution.py:303
  (32 shorter events, 0.1 us)
Async XLA Ops:
  8.3 25.7 %collective-permute-start = (bf16[32,16,128]{2,1,0:T(8,128)(2,1)}, bf16[32,16,128]{2,1,0:T(8,128)(2,1)S(1)}, u32[]{:S(2)}, u32[]{:S(2)}) collective-permute-start(bf16[32,16,128]{2,1,0:T(8,128)(2,1)} %get-tuple-element.24), channel_id=1, source_target_pairs={{0,8},{1,9},{2,10},{3,11},{4,12},{5,13},{6,14},{7,15},{8,0},{9,1},... | collective-permute-start | bytes 393224 | tf_op jit(solution)/shard_map/ppermute | solution.py:328
  11.5 24.8 %collective-permute-start.1 = (bf16[32,16,128]{2,1,0:T(8,128)(2,1)}, bf16[32,16,128]{2,1,0:T(8,128)(2,1)S(1)}, u32[]{:S(2)}, u32[]{:S(2)}) collective-permute-start(bf16[32,16,128]{2,1,0:T(8,128)(2,1)} %get-tuple-element.25), channel_id=1, source_target_pairs={{0,9},{1,8},{2,11},{3,10},{4,13},{5,12},{6,15},{7,14},{8,1},{9,0},... | collective-permute-start | bytes 393224 | tf_op jit(solution)/shard_map/ppermute | solution.py:328
  12.1 24.7 %collective-permute-start.2 = (bf16[32,16,128]{2,1,0:T(8,128)(2,1)}, bf16[32,16,128]{2,1,0:T(8,128)(2,1)S(1)}, u32[]{:S(2)}, u32[]{:S(2)}) collective-permute-start(bf16[32,16,128]{2,1,0:T(8,128)(2,1)} %get-tuple-element.26), channel_id=1, source_target_pairs={{0,10},{1,11},{2,8},{3,9},{4,14},{5,15},{6,12},{7,13},{8,2},{9,3},... | collective-permute-start | bytes 393224 | tf_op jit(solution)/shard_map/ppermute | solution.py:328
  18.2 49.8 %copy-start = (f32[4096]{0:T(1024)S(1)}, f32[4096]{0:T(1024)}, u32[]{:S(2)}) copy-start(f32[4096]{0:T(1024)} %param.15) | copy-start | bytes 49156
  32.4 34.6 %collective-permute-start.6 = (bf16[65,16,128]{2,1,0:T(8,128)(2,1)}, bf16[65,16,128]{2,1,0:T(8,128)(2,1)S(1)}, u32[]{:S(2)}, u32[]{:S(2)}) collective-permute-start(bf16[65,16,128]{2,1,0:T(8,128)(2,1)} %get-tuple-element.30), channel_id=1, source_target_pairs={{0,3},{1,2},{2,1},{3,0},{4,7},{5,6},{6,5},{7,4},{8,11},{9,10},{10,... | collective-permute-start | bytes 798728 | tf_op jit(solution)/shard_map/ppermute | solution.py:328
  32.4 34.6 %collective-permute-start.7 = (bf16[65,16,128]{2,1,0:T(8,128)(2,1)}, bf16[65,16,128]{2,1,0:T(8,128)(2,1)S(1)}, u32[]{:S(2)}, u32[]{:S(2)}) collective-permute-start(bf16[65,16,128]{2,1,0:T(8,128)(2,1)} %get-tuple-element.31), channel_id=1, source_target_pairs={{0,11},{1,10},{2,9},{3,8},{4,15},{5,14},{6,13},{7,12},{8,3},{9,2},... | collective-permute-start | bytes 798728 | tf_op jit(solution)/shard_map/ppermute | solution.py:328
  34.0 57.9 %copy-start.16 = (bf16[32,16,128]{2,1,0:T(8,128)(2,1)}, bf16[32,16,128]{2,1,0:T(8,128)(2,1)S(1)}, u32[]{:S(2)}) copy-start(bf16[32,16,128]{2,1,0:T(8,128)(2,1)S(1)} %collective-permute-done.rest_0_) | copy-start | bytes 393220
  34.0 26.7 %collective-permute-start.3 = (bf16[33,16,128]{2,1,0:T(8,128)(2,1)}, bf16[33,16,128]{2,1,0:T(8,128)(2,1)S(1)}, u32[]{:S(2)}, u32[]{:S(2)}) collective-permute-start(bf16[33,16,128]{2,1,0:T(8,128)(2,1)} %get-tuple-element.27), channel_id=1, source_target_pairs={{0,8},{1,9},{2,10},{3,11},{4,12},{5,13},{6,14},{7,15},{8,0},{9,1},... | collective-permute-start | bytes 405512 | tf_op jit(solution)/shard_map/ppermute | solution.py:328
  36.3 55.6 %copy-start.17 = (bf16[32,16,128]{2,1,0:T(8,128)(2,1)}, bf16[32,16,128]{2,1,0:T(8,128)(2,1)S(1)}, u32[]{:S(2)}) copy-start(bf16[32,16,128]{2,1,0:T(8,128)(2,1)S(1)} %collective-permute-done.1.rest_1_) | copy-start | bytes 393220
  36.3 27.3 %collective-permute-start.4 = (bf16[33,16,128]{2,1,0:T(8,128)(2,1)}, bf16[33,16,128]{2,1,0:T(8,128)(2,1)S(1)}, u32[]{:S(2)}, u32[]{:S(2)}) collective-permute-start(bf16[33,16,128]{2,1,0:T(8,128)(2,1)} %get-tuple-element.28), channel_id=1, source_target_pairs={{0,9},{1,8},{2,11},{3,10},{4,13},{5,12},{6,15},{7,14},{8,1},{9,0},... | collective-permute-start | bytes 405512 | tf_op jit(solution)/shard_map/ppermute | solution.py:328
  36.8 55.1 %copy-start.18 = (bf16[32,16,128]{2,1,0:T(8,128)(2,1)}, bf16[32,16,128]{2,1,0:T(8,128)(2,1)S(1)}, u32[]{:S(2)}) copy-start(bf16[32,16,128]{2,1,0:T(8,128)(2,1)S(1)} %collective-permute-done.2.rest_2_) | copy-start | bytes 393220
  36.8 29.5 %collective-permute-start.5 = (bf16[33,16,128]{2,1,0:T(8,128)(2,1)}, bf16[33,16,128]{2,1,0:T(8,128)(2,1)S(1)}, u32[]{:S(2)}, u32[]{:S(2)}) collective-permute-start(bf16[33,16,128]{2,1,0:T(8,128)(2,1)} %get-tuple-element.29), channel_id=1, source_target_pairs={{0,10},{1,11},{2,8},{3,9},{4,14},{5,15},{6,12},{7,13},{8,2},{9,3},... | collective-permute-start | bytes 405512 | tf_op jit(solution)/shard_map/ppermute | solution.py:328
  60.7 31.2 %copy-start.13 = (bf16[33,16,128]{2,1,0:T(8,128)(2,1)}, bf16[33,16,128]{2,1,0:T(8,128)(2,1)S(1)}, u32[]{:S(2)}) copy-start(bf16[33,16,128]{2,1,0:T(8,128)(2,1)S(1)} %collective-permute-done.3.rest_3_) | copy-start | bytes 405508
  60.7 11.3 %collective-permute-start.8 = (bf16[65,16,128]{2,1,0:T(8,128)(2,1)}, bf16[65,16,128]{2,1,0:T(8,128)(2,1)S(1)}, u32[]{:S(2)}, u32[]{:S(2)}) collective-permute-start(bf16[65,16,128]{2,1,0:T(8,128)(2,1)} %get-tuple-element.32), channel_id=1, source_target_pairs={{0,2},{1,3},{2,0},{3,1},{4,6},{5,7},{6,4},{7,5},{8,10},{9,11},{10,... | collective-permute-start | bytes 798728 | tf_op jit(solution)/shard_map/ppermute | solution.py:328
  63.6 28.3 %copy-start.14 = (bf16[33,16,128]{2,1,0:T(8,128)(2,1)}, bf16[33,16,128]{2,1,0:T(8,128)(2,1)S(1)}, u32[]{:S(2)}) copy-start(bf16[33,16,128]{2,1,0:T(8,128)(2,1)S(1)} %collective-permute-done.4.rest_4_) | copy-start | bytes 405508
  63.6 9.7 %collective-permute-start.9 = (bf16[65,16,128]{2,1,0:T(8,128)(2,1)}, bf16[65,16,128]{2,1,0:T(8,128)(2,1)S(1)}, u32[]{:S(2)}, u32[]{:S(2)}) collective-permute-start(bf16[65,16,128]{2,1,0:T(8,128)(2,1)} %get-tuple-element.33), channel_id=1, source_target_pairs={{0,12},{1,13},{2,14},{3,15},{4,8},{5,9},{6,10},{7,11},{8,4},{9,5},... | collective-permute-start | bytes 798728 | tf_op jit(solution)/shard_map/ppermute | solution.py:328
  66.3 25.6 %copy-start.15 = (bf16[33,16,128]{2,1,0:T(8,128)(2,1)}, bf16[33,16,128]{2,1,0:T(8,128)(2,1)S(1)}, u32[]{:S(2)}) copy-start(bf16[33,16,128]{2,1,0:T(8,128)(2,1)S(1)} %collective-permute-done.5.rest_5_) | copy-start | bytes 405508
  66.3 11.7 %collective-permute-start.10 = (bf16[65,16,128]{2,1,0:T(8,128)(2,1)}, bf16[65,16,128]{2,1,0:T(8,128)(2,1)S(1)}, u32[]{:S(2)}, u32[]{:S(2)}) collective-permute-start(bf16[65,16,128]{2,1,0:T(8,128)(2,1)} %get-tuple-element.34), channel_id=1, source_target_pairs={{0,1},{1,0},{2,3},{3,2},{4,5},{5,4},{6,7},{7,6},{8,9},{9,8},{10,11... | collective-permute-start | bytes 798728 | tf_op jit(solution)/shard_map/ppermute | solution.py:328
  67.0 24.9 %copy-start.1 = (bf16[65,16,128]{2,1,0:T(8,128)(2,1)}, bf16[65,16,128]{2,1,0:T(8,128)(2,1)S(1)}, u32[]{:S(2)}) copy-start(bf16[65,16,128]{2,1,0:T(8,128)(2,1)S(1)} %collective-permute-done.6.rest_6_) | copy-start | bytes 798724
  67.0 13.6 %collective-permute-start.11 = (bf16[65,16,128]{2,1,0:T(8,128)(2,1)}, bf16[65,16,128]{2,1,0:T(8,128)(2,1)S(1)}, u32[]{:S(2)}, u32[]{:S(2)}) collective-permute-start(bf16[65,16,128]{2,1,0:T(8,128)(2,1)} %get-tuple-element.35), channel_id=1, source_target_pairs={{0,4},{1,5},{2,6},{3,7},{4,0},{5,1},{6,2},{7,3},{8,12},{9,13},{10,... | collective-permute-start | bytes 798728 | tf_op jit(solution)/shard_map/ppermute | solution.py:328
  67.0 24.9 %copy-start.2 = (bf16[65,16,128]{2,1,0:T(8,128)(2,1)}, bf16[65,16,128]{2,1,0:T(8,128)(2,1)S(1)}, u32[]{:S(2)}) copy-start(bf16[65,16,128]{2,1,0:T(8,128)(2,1)S(1)} %collective-permute-done.7.rest_7_) | copy-start | bytes 798724
  67.0 19.1 %collective-permute-start.12 = (bf16[65,16,128]{2,1,0:T(8,128)(2,1)}, bf16[65,16,128]{2,1,0:T(8,128)(2,1)S(1)}, u32[]{:S(2)}, u32[]{:S(2)}) collective-permute-start(bf16[65,16,128]{2,1,0:T(8,128)(2,1)} %get-tuple-element.36), channel_id=1, source_target_pairs={{0,13},{1,12},{2,15},{3,14},{4,9},{5,8},{6,11},{7,10},{8,5},{9,4},... | collective-permute-start | bytes 798728 | tf_op jit(solution)/shard_map/ppermute | solution.py:328
  72.0 20.0 %copy-start.3 = (bf16[65,16,128]{2,1,0:T(8,128)(2,1)}, bf16[65,16,128]{2,1,0:T(8,128)(2,1)S(1)}, u32[]{:S(2)}) copy-start(bf16[65,16,128]{2,1,0:T(8,128)(2,1)S(1)} %collective-permute-done.8.rest_8_) | copy-start | bytes 798724
  72.0 20.0 %collective-permute-start.13 = (bf16[65,16,128]{2,1,0:T(8,128)(2,1)}, bf16[65,16,128]{2,1,0:T(8,128)(2,1)S(1)}, u32[]{:S(2)}, u32[]{:S(2)}) collective-permute-start(bf16[65,16,128]{2,1,0:T(8,128)(2,1)} %get-tuple-element.37), channel_id=1, source_target_pairs={{0,5},{1,4},{2,7},{3,6},{4,1},{5,0},{6,3},{7,2},{8,13},{9,12},{10,... | collective-permute-start | bytes 798728 | tf_op jit(solution)/shard_map/ppermute | solution.py:328
  73.3 18.7 %copy-start.4 = (bf16[65,16,128]{2,1,0:T(8,128)(2,1)}, bf16[65,16,128]{2,1,0:T(8,128)(2,1)S(1)}, u32[]{:S(2)}) copy-start(bf16[65,16,128]{2,1,0:T(8,128)(2,1)S(1)} %collective-permute-done.9.rest_9_) | copy-start | bytes 798724
  73.3 23.8 %collective-permute-start.14 = (bf16[65,16,128]{2,1,0:T(8,128)(2,1)}, bf16[65,16,128]{2,1,0:T(8,128)(2,1)S(1)}, u32[]{:S(2)}, u32[]{:S(2)}) collective-permute-start(bf16[65,16,128]{2,1,0:T(8,128)(2,1)} %get-tuple-element.38), channel_id=1, source_target_pairs={{0,6},{1,7},{2,4},{3,5},{4,2},{5,3},{6,0},{7,1},{8,14},{9,15},{10,... | collective-permute-start | bytes 798728 | tf_op jit(solution)/shard_map/ppermute | solution.py:328
  78.0 14.0 %copy-start.5 = (bf16[65,16,128]{2,1,0:T(8,128)(2,1)}, bf16[65,16,128]{2,1,0:T(8,128)(2,1)S(1)}, u32[]{:S(2)}) copy-start(bf16[65,16,128]{2,1,0:T(8,128)(2,1)S(1)} %collective-permute-done.10.rest_10_) | copy-start | bytes 798724
  78.0 27.3 %collective-permute-start.15 = (bf16[65,16,128]{2,1,0:T(8,128)(2,1)}, bf16[65,16,128]{2,1,0:T(8,128)(2,1)S(1)}, u32[]{:S(2)}, u32[]{:S(2)}) collective-permute-start(bf16[65,16,128]{2,1,0:T(8,128)(2,1)} %get-tuple-element.39), channel_id=1, source_target_pairs={{0,14},{1,15},{2,12},{3,13},{4,10},{5,11},{6,8},{7,9},{8,6},{9,7},... | collective-permute-start | bytes 798728 | tf_op jit(solution)/shard_map/ppermute | solution.py:328
  80.6 11.4 %copy-start.6 = (bf16[65,16,128]{2,1,0:T(8,128)(2,1)}, bf16[65,16,128]{2,1,0:T(8,128)(2,1)S(1)}, u32[]{:S(2)}) copy-start(bf16[65,16,128]{2,1,0:T(8,128)(2,1)S(1)} %collective-permute-done.11.rest_11_) | copy-start | bytes 798724
  80.6 31.0 %collective-permute-start.16 = (bf16[65,16,128]{2,1,0:T(8,128)(2,1)}, bf16[65,16,128]{2,1,0:T(8,128)(2,1)S(1)}, u32[]{:S(2)}, u32[]{:S(2)}) collective-permute-start(bf16[65,16,128]{2,1,0:T(8,128)(2,1)} %get-tuple-element.40), channel_id=1, source_target_pairs={{0,7},{1,6},{2,5},{3,4},{4,3},{5,2},{6,1},{7,0},{8,15},{9,14},{10,... | collective-permute-start | bytes 798728 | tf_op jit(solution)/shard_map/ppermute | solution.py:328
  86.1 5.9 %copy-start.7 = (bf16[65,16,128]{2,1,0:T(8,128)(2,1)}, bf16[65,16,128]{2,1,0:T(8,128)(2,1)S(1)}, u32[]{:S(2)}) copy-start(bf16[65,16,128]{2,1,0:T(8,128)(2,1)S(1)} %collective-permute-done.12.rest_12_) | copy-start | bytes 798724
  86.1 34.2 %collective-permute-start.17 = (bf16[65,16,128]{2,1,0:T(8,128)(2,1)}, bf16[65,16,128]{2,1,0:T(8,128)(2,1)S(1)}, u32[]{:S(2)}, u32[]{:S(2)}) collective-permute-start(bf16[65,16,128]{2,1,0:T(8,128)(2,1)} %get-tuple-element.41), channel_id=1, source_target_pairs={{0,15},{1,14},{2,13},{3,12},{4,11},{5,10},{6,9},{7,8},{8,7},{9,6},... | collective-permute-start | bytes 798728 | tf_op jit(solution)/shard_map/ppermute | solution.py:328
  92.0 28.3 %copy-start.8 = (bf16[65,16,128]{2,1,0:T(8,128)(2,1)}, bf16[65,16,128]{2,1,0:T(8,128)(2,1)S(1)}, u32[]{:S(2)}) copy-start(bf16[65,16,128]{2,1,0:T(8,128)(2,1)S(1)} %collective-permute-done.13.rest_13_) | copy-start | bytes 798724
  97.1 23.3 %copy-start.9 = (bf16[65,16,128]{2,1,0:T(8,128)(2,1)}, bf16[65,16,128]{2,1,0:T(8,128)(2,1)S(1)}, u32[]{:S(2)}) copy-start(bf16[65,16,128]{2,1,0:T(8,128)(2,1)S(1)} %collective-permute-done.14.rest_14_) | copy-start | bytes 798724
  105.3 15.0 %copy-start.10 = (bf16[65,16,128]{2,1,0:T(8,128)(2,1)}, bf16[65,16,128]{2,1,0:T(8,128)(2,1)S(1)}, u32[]{:S(2)}) copy-start(bf16[65,16,128]{2,1,0:T(8,128)(2,1)S(1)} %collective-permute-done.15.rest_15_) | copy-start | bytes 798724
  111.6 8.8 %copy-start.11 = (bf16[65,16,128]{2,1,0:T(8,128)(2,1)}, bf16[65,16,128]{2,1,0:T(8,128)(2,1)S(1)}, u32[]{:S(2)}) copy-start(bf16[65,16,128]{2,1,0:T(8,128)(2,1)S(1)} %collective-permute-done.16.rest_16_) | copy-start | bytes 798724
  120.3 0.7 copy-start.12
where the time goes:
time: 131 us
  waiting for transfers between devices  65.6 us (50%)
  Pallas kernels  38.2 us (29%)
  starting transfers between devices  23 us (18%)
  between operations  2.29 us (2%)
  local copies, waits for them, and re-layouts  1.43 us (1%)
    ppermute x18, waiting for transfers between devices, exchange(): return lax.ppermute(piece, 'facet', [(i, i ^ s) for i in range(16)])  65.6 us
    ppermute x18, starting transfers between devices, exchange(): return lax.ppermute(piece, 'facet', [(i, i ^ s) for i in range(16)])  23 us
    pallas_call x2, Pallas kernels, forward(): pl.pallas_call(functools.partial(forward_kernel, subset=subset, starts=st...  22.5 us
    pallas_call x1, Pallas kernels, final(): pl.pallas_call(functools.partial(final_kernel, sizes=sizes), in_specs=[hb...  9.91 us
    pallas_call x1, Pallas kernels, scale(): pl.pallas_call(scale_kernel, grid=(1,), in_specs=[whole(correction.shape)...  5.8 us
  transfers between devices with their start and end apart: 18, of which 11 were waited for; matrix products, arithmetic and copies ran while one was open for 1% of the time, Pallas kernels for 15%

commit v1 on v0

--- a/solution.py
+++ b/solution.py
@@ -54,12 +54,13 @@
     return table.reshape(64, 128, 128)
 
 
-def forward_kernel(*rest, subset, starts, count, extra):
+def forward_kernel(*rest, near, subset, starts, count, extra):
     if extra:
         meta_ref, *rest = rest
     sub_hbm, taper_ref, first_hbm, second_ref, *rest = rest
-    outs = rest[: len(subset)]
-    sub_ref, first_ref, plain, tapers, mid, pieces, sub_sem, first_sem, out_sem = rest[len(subset) :]
+    number = near + len(subset)
+    outs = rest[: len(subset) + (1 if near else 0)]
+    sub_ref, first_ref, plain, tapers, mid, pieces, sub_sem, first_sem, out_sem = rest[len(outs) :]
     sub_copies, first_copies, out_copies = [], [], []
     for q in range(4):
         for x in range(2):
@@ -117,15 +118,16 @@
                 mid[pl.ds(128 + b, count, stride=PITCH_MID), :] = mine[count:]
 
     me = lax.axis_index("facet")
-    blocks = [pl.ds(pl.multiple_of((me ^ s) * 16, 16), 16) for s in subset]
+    facets = [(me // 8) * 8 + j for j in range(near)] + [me ^ s for s in subset]
+    blocks = [pl.ds(pl.multiple_of(f * 16, 16), 16) for f in facets]
     high = jnp.concatenate([second_ref[rows, 0:256] for rows in blocks], axis=0)
     low = jnp.concatenate([second_ref[rows, 256:512] for rows in blocks], axis=0)
-    rows = 16 * len(subset)
+    rows = 16 * number
     if extra:
         row = lax.broadcasted_iota(jnp.int32, (16, 128), 0)
         tile = jnp.where(row == 0, meta_ref[0], jnp.where(row == 1, meta_ref[1], meta_ref[2]))
         tile = tile.astype(f32).astype(bf16)
-        for i in range(len(subset)):
+        for i in range(number):
             pieces[i, count] = tile
     part = count // 2
     for half in range(2):
@@ -140,16 +142,23 @@
             out = jnp.dot(jnp.concatenate([high, low], axis=0), data_high, preferred_element_type=f32)
             out = out[:rows] + out[rows:] + jnp.dot(high, data_low, preferred_element_type=f32)
             out = out.astype(bf16)
-            for i in range(len(subset)):
+            for i in range(number):
                 for j in range(2):
                     pieces[i, 2 * pair + j] = out[i * 16 : i * 16 + 16, j * 128 : j * 128 + 128]
 
         size = part + (extra if half else 0)
+        span = pl.ds(half * part, size)
+        if near:
+            copy = pltpu.make_async_copy(
+                pieces.at[pl.ds(0, near), span], outs[0].at[:, span], out_sem.at[half, len(subset)]
+            )
+            copy.start()
+            out_copies.append(copy)
         for i, start in enumerate(starts):
             if half * part >= start:
                 copy = pltpu.make_async_copy(
-                    pieces.at[i, pl.ds(half * part, size)],
-                    outs[i].at[pl.ds(half * part - start, size)],
+                    pieces.at[near + i, span],
+                    outs[len(outs) - len(subset) + i].at[pl.ds(half * part - start, size)],
                     out_sem.at[half, i],
                 )
                 copy.start()
@@ -158,12 +167,15 @@
         copy.wait()
 
 
-def forward(subgrid, taper, first, second, subset, starts, meta=None):
-    number, count, extra = len(subset), first.shape[1], 0 if meta is None else 1
-    shapes = [jax.ShapeDtypeStruct((count - start + extra, 16, 128), bf16) for start in starts]
+def forward(subgrid, taper, first, second, near, subset, starts, meta=None):
+    number, count, extra = near + len(subset), first.shape[1], 0 if meta is None else 1
+    shapes = [jax.ShapeDtypeStruct((near, count + extra, 16, 128), bf16)] * (1 if near else 0)
+    shapes += [jax.ShapeDtypeStruct((count - start + extra, 16, 128), bf16) for start in starts]
     hbm = pl.BlockSpec(memory_space=pl.ANY)
     return pl.pallas_call(
-        functools.partial(forward_kernel, subset=subset, starts=starts, count=count, extra=extra),
+        functools.partial(
+            forward_kernel, near=near, subset=subset, starts=starts, count=count, extra=extra
+        ),
         grid=(1,),
         in_specs=[pl.BlockSpec(memory_space=pltpu.SMEM)] * extra
         + [
@@ -172,7 +184,7 @@
             hbm,
             pl.BlockSpec((256, 512), lambda i: (0, 0)),
         ],
-        out_specs=[hbm] * number,
+        out_specs=[hbm] * len(shapes),
         out_shape=shapes,
         scratch_shapes=[
             pltpu.VMEM((2, 8192, 128), bf16),
@@ -183,7 +195,7 @@
             pltpu.VMEM((number, count + extra, 16, 128), bf16),
             pltpu.SemaphoreType.DMA((4, 2)),
             pltpu.SemaphoreType.DMA((4,)),
-            pltpu.SemaphoreType.DMA((2, number)),
+            pltpu.SemaphoreType.DMA((2, len(subset) + 1)),
         ],
         compiler_params=pltpu.CompilerParams(vmem_limit_bytes=58 * MIB),
         cost_estimate=pl.CostEstimate(flops=160000000 * count, bytes_accessed=12 * MIB, transcendentals=0),
@@ -234,26 +246,27 @@
     )(correction, table)
 
 
-def final_kernel(scaled_hbm, *rest, sizes):
-    refs = rest[: len(sizes)]
-    out_hbm, store, held, scaled_ref, image, piece_sem, scaled_sem, out_sem = rest[len(sizes) :]
+def final_kernel(scaled_hbm, *rest, early, far):
+    halves, near_ref, wholes = rest[:early], rest[early], rest[early + 1 : early + 1 + far]
+    out_hbm, store, held, scaled_ref, image, piece_sem, scaled_sem, out_sem = rest[early + 1 + far :]
     scaled_copies, out_copies = [], []
     piece_copies = [[], [], []]
-
-    def fetch(ref, at, s, stage, start, size):
-        target = held.at[s, pl.ds(start, size)]
-        copy = pltpu.make_async_copy(ref.at[pl.ds(at, size)], target, piece_sem.at[stage, s])
+    near = near_ref.shape[0]
+
+    def fetch(source, target, stage, index):
+        copy = pltpu.make_async_copy(source, target, piece_sem.at[stage, index])
         copy.start()
         piece_copies[stage].append(copy)
 
-    wholes = refs[len(sizes) - 16 :]
-    halves = refs[: len(sizes) - 16]
-    for s, ref in enumerate(wholes):
-        fetch(ref, ref.shape[0] - 1, s, 0, 64, 1)
-    for s, ref in enumerate(wholes):
-        fetch(halves[s] if s < len(halves) else ref, 0, s, 1, 0, 32)
-    for s, ref in enumerate(wholes):
-        fetch(ref, 0 if s < len(halves) else 32, s, 2, 32, 32)
+    for stage, start, size in ((0, 64, 1), (1, 0, 32), (2, 32, 32)):
+        span = pl.ds(start, size)
+        fetch(near_ref.at[:, span], held.at[pl.ds(0, near), span], stage, far)
+        for i, whole in enumerate(wholes):
+            if i < early and stage == 1:
+                source = halves[i]
+            else:
+                source = whole.at[pl.ds(start - (32 if i < early else 0), size)]
+            fetch(source, held.at[near + i, span], stage, i)
     for q in range(4):
         part = pl.ds(16 * q, 16)
         copy = pltpu.make_async_copy(scaled_hbm.at[part], scaled_ref.at[part], scaled_sem.at[q])
@@ -297,11 +310,11 @@
         copy.wait()
 
 
-def final(scaled, pieces):
+def final(scaled, early, near, far):
     hbm = pl.BlockSpec(memory_space=pl.ANY)
-    sizes = tuple(piece.shape[0] for piece in pieces)
+    pieces = early + [near] + far
     return pl.pallas_call(
-        functools.partial(final_kernel, sizes=sizes),
+        functools.partial(final_kernel, early=len(early), far=len(far)),
         in_specs=[hbm] * (1 + len(pieces)),
         out_specs=hbm,
         out_shape=jax.ShapeDtypeStruct((2, 2, 64, 64, 128), f32),
@@ -310,7 +323,7 @@
             pltpu.VMEM((16, 65, 16, 128), bf16),
             pltpu.VMEM((64, 128, 256), bf16),
             pltpu.VMEM((4 * 64 * PITCH_IMAGE, 128), f32),
-            pltpu.SemaphoreType.DMA((3, 16)),
+            pltpu.SemaphoreType.DMA((3, len(far) + 1)),
             pltpu.SemaphoreType.DMA((4,)),
             pltpu.SemaphoreType.DMA((2, 2)),
         ],
@@ -320,8 +333,9 @@
     )(scaled, *pieces)
 
 
-EARLY = (8, 9, 10)
-LATE = (8, 9, 10, 3, 11, 2, 12, 1, 4, 13, 5, 6, 14, 7, 15)
+NEAR = 8
+EARLY = (8, 9, 10, 11)
+FAR = (8, 9, 10, 11, 12, 13, 14, 15)
 
 
 def exchange(piece, s):
@@ -331,14 +345,16 @@
 def local(subgrids, taper, counts, positions, channels, correction):
     first, second = forward_tables()
     inputs = (subgrids[0], taper.reshape(64, 128))
-    early = forward(*inputs, first[:, :32], second, EARLY, (0,) * len(EARLY))
-    starts = tuple(32 if s in EARLY else 0 for s in LATE) + (0,)
+    early = forward(*inputs, first[:, :32], second, 0, EARLY, (0,) * len(EARLY))
+    starts = tuple(32 if s in EARLY else 0 for s in FAR)
     meta = jnp.concatenate([counts, positions, channels])
-    late = forward(*inputs, first, second, LATE + (0,), starts, meta)
+    near, *far = forward(*inputs, first, second, NEAR, FAR, starts, meta)
     early = [exchange(piece, s) for s, piece in zip(EARLY, early)]
-    late = [exchange(piece, s) for s, piece in zip(LATE, late)] + [late[15]]
+    far = [exchange(piece, s) for s, piece in zip(FAR, far)]
+    halves = [list(range(NEAR)), list(range(NEAR, 2 * NEAR))]
+    near = lax.all_to_all(near, "facet", split_axis=0, concat_axis=0, axis_index_groups=halves, tiled=True)
     scaled = scale(correction.reshape(64, 64), inverse_table())
-    image = final(scaled, early + late)
+    image = final(scaled, early, near, far)
     return image.reshape(TAYLOR, 2, 4096, 128)
 
 

time: 131 us -> 139 us (1.061)
  the two profiles are of different devices: /device:TPU:1 before, /device:TPU:13 now
where the time goes in v1:
time: 139 us; the launch traced here: 138 us
  waiting for transfers between devices  70.5 us (51%)
  Pallas kernels  37.6 us (27%)
  starting transfers between devices  23.5 us (17%)
  local copies, waits for them, and re-layouts  3.43 us (2%)
  between operations  2.19 us (2%)
    ppermute x12, waiting for transfers between devices, exchange(): return lax.ppermute(piece, 'facet', [(i, i ^ s) for i in range(16)])  70.5 us
    pallas_call x2, Pallas kernels, forward(): pl.pallas_call(functools.partial(forward_kernel, near=near, subset=subset...  22.3 us
    ppermute x12, starting transfers between devices, exchange(): return lax.ppermute(piece, 'facet', [(i, i ^ s) for i in range(16)])  19 us
    pallas_call x1, Pallas kernels, final(): pl.pallas_call(functools.partial(final_kernel, early=len(early), far=len(...  9.62 us
    pallas_call x1, Pallas kernels, scale(): pl.pallas_call(scale_kernel, grid=(1,), in_specs=[whole(correction.shape)...  5.68 us
    all_to_all x1, starting transfers between devices, local(): lax.all_to_all(near, 'facet', split_axis=0, concat_axis=0, axis_index_gro...  4.52 us
  transfers between devices with their start and end apart: 13, of which 8 were waited for; matrix products, arithmetic and copies ran while one was open for 0% of the time, Pallas kernels for 10%

profile of v1, /device:TPU:13, one launch (start us, length us, event | category | flops | bytes accessed | tf_op | source)
XLA Modules:
  0.0 138.0 jit_solution(583506796410326371)
XLA Ops:
  1.9 0.7 pad_add_fusion.rest_0_
  2.6 13.8 %forward16.1 = (bf16[8,65,16,128]{3,2,1,0:T(8,128)(2,1)}, bf16[33,16,128]{2,1,0:T(8,128)(2,1)}, bf16[33,16,128]{2,1,0:T(8,128)(2,1)}, bf16[33,16,128]{2,1,0:T(8,...) custom-call(s32[3]{0:T(128)} %pad_add_fusion.rest_0_, ...), custom_call_target="tpu_custom_call" | custom-call | flops 10240000000 | bytes 12582912 | tf_op jit(solution)/shard_map/forward16/pallas_call | solution.py:175
  16.4 4.5 %all-to-all-start = ((bf16[8,65,16,128]{3,2,1,0:T(8,128)(2,1)}), bf16[8,65,16,128]{3,2,1,0:T(8,128)(2,1)S(1)}, u32[]{:S(2)}, u32[]{:S(2)}) async-start(bf16[8,65,16,128]{3,2,1,0:T(8,128)(2,1)} %get-tuple-element.22), calls=%async_computation | async-start | bytes 4259840 | tf_op jit(solution)/shard_map/all_to_all | solution.py:355
  21.0 0.0 copy-start.1
  21.0 0.0 copy-start.5
  21.0 0.0 copy-start.3
  21.0 0.0 copy-start.2
  21.0 8.5 %forward4.1 = (bf16[32,16,128]{2,1,0:T(8,128)(2,1)}, bf16[32,16,128]{2,1,0:T(8,128)(2,1)}, bf16[32,16,128]{2,1,0:T(8,128)(2,1)}, bf16[32,16,128]{2,1,0:T(8,128)(2,1)}) custom-call(bf16[2,8192,128]{2,1,0:T(8,128)(2,1)} %bitcast.4, f32[64,128]{1,0:T(8,128)} %bitcast.6, f32[128,32,128]{2,1,0:T(8,128)} %constant.8.clone.rest_2_, ...), custom_call_target="tpu_custom_call" | custom-call | flops 5120000000 | bytes 12582912 | tf_op jit(solution)/shard_map/forward4/pallas_call | solution.py:175
  29.5 2.4 %collective-permute-start = (bf16[32,16,128]{2,1,0:T(8,128)(2,1)}, bf16[32,16,128]{2,1,0:T(8,128)(2,1)}, u32[]{:S(2)}, u32[]{:S(2)}) collective-permute-start(bf16[32,16,128]{2,1,0:T(8,128)(2,1)} %get-tuple-element.18), channel_id=1, source_target_pairs={{0,8},{1,9},{2,10},{3,11},{4,12},{5,13},{6,14},{7,15},{8,0},{9,1},... | collective-permute-start | bytes 393224 | tf_op jit(solution)/shard_map/ppermute | solution.py:342
  31.9 0.6 collective-permute-start.1
  32.4 2.3 %collective-permute-start.4 = (bf16[33,16,128]{2,1,0:T(8,128)(2,1)}, bf16[33,16,128]{2,1,0:T(8,128)(2,1)}, u32[]{:S(2)}, u32[]{:S(2)}) collective-permute-start(bf16[33,16,128]{2,1,0:T(8,128)(2,1)} %get-tuple-element.23), channel_id=1, source_target_pairs={{0,8},{1,9},{2,10},{3,11},{4,12},{5,13},{6,14},{7,15},{8,0},{9,1},... | collective-permute-start | bytes 405512 | tf_op jit(solution)/shard_map/ppermute | solution.py:342
  34.8 0.3 collective-permute-start.5
  35.1 2.1 %collective-permute-start.6 = (bf16[33,16,128]{2,1,0:T(8,128)(2,1)}, bf16[33,16,128]{2,1,0:T(8,128)(2,1)}, u32[]{:S(2)}, u32[]{:S(2)}) collective-permute-start(bf16[33,16,128]{2,1,0:T(8,128)(2,1)} %get-tuple-element.25), channel_id=1, source_target_pairs={{0,10},{1,11},{2,8},{3,9},{4,14},{5,15},{6,12},{7,13},{8,2},{9,3},... | collective-permute-start | bytes 405512 | tf_op jit(solution)/shard_map/ppermute | solution.py:342
  37.2 12.8 %collective-permute-done.rest_0_ = bf16[32,16,128]{2,1,0:T(8,128)(2,1)} collective-permute-done((bf16[32,16,128]{2,1,0:T(8,128)(2,1)}, bf16[32,16,128]{2,1,0:T(8,128)(2,1)}, u32[]{:S(2)}, u32[]{:S(2)}) %collective-permute-start) | collective-permute-done | bytes 131104 | tf_op jit(solution)/shard_map/ppermute | solution.py:342
  50.0 0.0 collective-permute-start.2
  50.0 3.6 %collective-permute-done.1.rest_1_ = bf16[32,16,128]{2,1,0:T(8,128)(2,1)} collective-permute-done((bf16[32,16,128]{2,1,0:T(8,128)(2,1)}, bf16[32,16,128]{2,1,0:T(8,128)(2,1)}, u32[]{:S(2)}, u32[]{:S(2)}) %collective-permute-start.1) | collective-permute-done | bytes 131104 | tf_op jit(solution)/shard_map/ppermute | solution.py:342
  53.5 1.2 collective-permute-start.3
  54.8 0.0 copy-done.1
  54.8 0.7 reshape.9.correction_ref
  55.5 13.5 %collective-permute-done.2.rest_2_ = bf16[32,16,128]{2,1,0:T(8,128)(2,1)S(1)} collective-permute-done((bf16[32,16,128]{2,1,0:T(8,128)(2,1)}, bf16[32,16,128]{2,1,0:T(8,128)(2,1)S(1)}, u32[]{:S(2)}, u32[]{:S(2)}) %collective-permute-start.2) | collective-permute-done | bytes 131104 | tf_op jit(solution)/shard_map/ppermute | solution.py:342
  69.0 5.8 %collective-permute-start.7 = (bf16[33,16,128]{2,1,0:T(8,128)(2,1)}, bf16[33,16,128]{2,1,0:T(8,128)(2,1)S(1)}, u32[]{:S(2)}, u32[]{:S(2)}) collective-permute-start(bf16[33,16,128]{2,1,0:T(8,128)(2,1)} %get-tuple-element.26), channel_id=1, source_target_pairs={{0,11},{1,10},{2,9},{3,8},{4,15},{5,14},{6,13},{7,12},{8,3},{9,2},... | collective-permute-start | bytes 405512 | tf_op jit(solution)/shard_map/ppermute | solution.py:342
  74.7 0.0 collective-permute-done.3.rest_3_
  74.7 0.0 copy-done.10
  74.7 0.6 copy-done.11
  75.4 0.0 copy-done.5
  75.4 0.0 collective-permute-start.8
  75.4 0.0 collective-permute-done.4.rest_5_
  75.4 0.0 copy-done.4
  75.4 2.8 %collective-permute-start.9 = (bf16[65,16,128]{2,1,0:T(8,128)(2,1)S(1)}, bf16[65,16,128]{2,1,0:T(8,128)(2,1)S(1)}, u32[]{:S(2)}, u32[]{:S(2)}) collective-permute-start(bf16[65,16,128]{2,1,0:T(8,128)(2,1)S(1)} %copy-done.4), channel_id=1, source_target_pairs={{0,13},{1,12},{2,15},{3,14},{4,9},{5,8},{6,11},{7,10},{8,5},{9,4},... | collective-permute-start | bytes 798728 | tf_op jit(solution)/shard_map/ppermute | solution.py:342
  78.2 0.0 collective-permute-done.5.rest_6_
  78.2 0.0 copy-done.3
  78.2 0.0 collective-permute-start.10
  78.2 0.0 collective-permute-done.6.rest_7_
  78.2 0.0 copy-done.2
  78.2 1.6 %collective-permute-start.11 = (bf16[65,16,128]{2,1,0:T(8,128)(2,1)S(1)}, bf16[65,16,128]{2,1,0:T(8,128)(2,1)}, u32[]{:S(2)}, u32[]{:S(2)}) collective-permute-start(bf16[65,16,128]{2,1,0:T(8,128)(2,1)S(1)} %copy-done.2), channel_id=1, source_target_pairs={{0,15},{1,14},{2,13},{3,12},{4,11},{5,10},{6,9},{7,8},{8,7},{9,6},... | collective-permute-start | bytes 798728 | tf_op jit(solution)/shard_map/ppermute | solution.py:342
  79.8 5.7 %scale.1.scaled_hbm = bf16[64,128,256]{2,1,0:T(8,128)(2,1)} custom-call(f32[64,64]{1,0:T(8,128)} %reshape.9.correction_ref, f32[64,128,128]{2,1,0:T(8,128)} %constant.11.clone.table_ref), custom_call_target="tpu_custom_call" | custom-call | flops 6000000000 | bytes 16777216 | tf_op jit(solution)/shard_map/scale/pallas_call | solution.py:237
  85.5 15.9 %collective-permute-done.7.rest_8_ = bf16[33,16,128]{2,1,0:T(8,128)(2,1)S(1)} collective-permute-done((bf16[33,16,128]{2,1,0:T(8,128)(2,1)}, bf16[33,16,128]{2,1,0:T(8,128)(2,1)S(1)}, u32[]{:S(2)}, u32[]{:S(2)}) %collective-permute-start.7) | collective-permute-done | bytes 135200 | tf_op jit(solution)/shard_map/ppermute | solution.py:342
  101.3 7.6 %collective-permute-done.8.rest_9_ = bf16[65,16,128]{2,1,0:T(8,128)(2,1)S(1)} collective-permute-done((bf16[65,16,128]{2,1,0:T(8,128)(2,1)S(1)}, bf16[65,16,128]{2,1,0:T(8,128)(2,1)S(1)}, u32[]{:S(2)}, u32[]{:S(2)}) %collective-permute-start.8) | collective-permute-done | bytes 266272 | tf_op jit(solution)/shard_map/ppermute | solution.py:342
  109.0 5.7 %collective-permute-done.9.rest_10_ = bf16[65,16,128]{2,1,0:T(8,128)(2,1)S(1)} collective-permute-done((bf16[65,16,128]{2,1,0:T(8,128)(2,1)S(1)}, bf16[65,16,128]{2,1,0:T(8,128)(2,1)S(1)}, u32[]{:S(2)}, u32[]{:S(2)}) %collective-permute-start.9) | collective-permute-done | bytes 266272 | tf_op jit(solution)/shard_map/ppermute | solution.py:342
  114.7 6.3 %collective-permute-done.10.rest_11_ = bf16[65,16,128]{2,1,0:T(8,128)(2,1)S(1)} collective-permute-done((bf16[65,16,128]{2,1,0:T(8,128)(2,1)S(1)}, bf16[65,16,128]{2,1,0:T(8,128)(2,1)S(1)}, u32[]{:S(2)}, u32[]{:S(2)}) %collective-permute-start.10) | collective-permute-done | bytes 266272 | tf_op jit(solution)/shard_map/ppermute | solution.py:342
  121.0 0.0 copy-done.9
  121.0 0.0 copy-done.7
  121.0 0.7 copy-done.8
  121.7 5.1 %collective-permute-done.11.rest_12_ = bf16[65,16,128]{2,1,0:T(8,128)(2,1)} collective-permute-done((bf16[65,16,128]{2,1,0:T(8,128)(2,1)S(1)}, bf16[65,16,128]{2,1,0:T(8,128)(2,1)}, u32[]{:S(2)}, u32[]{:S(2)}) %collective-permute-start.11) | collective-permute-done | bytes 266272 | tf_op jit(solution)/shard_map/ppermute | solution.py:342
  126.8 0.0 all-to-all-done.rest_4_
  126.8 0.0 copy-done.6
  126.8 1.4 copy-done
  128.2 9.6 %final.1 = f32[2,2,64,64,128]{4,3,2,1,0:T(8,128)} custom-call(bf16[64,128,256]{2,1,0:T(8,128)(2,1)} %scale.1.scaled_hbm, bf16[32,16,128]{2,1,0:T(8,128)(2,1)} %collective-permute-done.rest_0_, bf16[32,16,128]{2,1,0:T(8,128)(2,1)} %collective-permute-done.1.rest_1_, bf16[32,16,128]{2,1,0:T(8,128)(2,1)} %copy-done.10, bf16[32,16,128]{2,1,0:T(8,128)(2,1)} %copy-done.11, ...), custom_call_target="tpu_custom_call" | custom-call | flops 8000000000 | bytes 16777216 | tf_op jit(solution)/shard_map/final/pallas_call | solution.py:316
  (8 shorter events, 0.0 us)
Async XLA Ops:
  16.4 110.4 %all-to-all-start = ((bf16[8,65,16,128]{3,2,1,0:T(8,128)(2,1)}), bf16[8,65,16,128]{3,2,1,0:T(8,128)(2,1)S(1)}, u32[]{:S(2)}, u32[]{:S(2)}) async-start(bf16[8,65,16,128]{3,2,1,0:T(8,128)(2,1)} %get-tuple-element.22), calls=%async_computation | async-start | bytes 4259840 | tf_op jit(solution)/shard_map/all_to_all | solution.py:355
  21.0 33.8 %copy-start.1 = (f32[4096]{0:T(1024)S(1)}, f32[4096]{0:T(1024)}, u32[]{:S(2)}) copy-start(f32[4096]{0:T(1024)} %param.15) | copy-start | bytes 49156
  21.0 54.4 %copy-start.5 = (bf16[65,16,128]{2,1,0:T(8,128)(2,1)S(1)}, bf16[65,16,128]{2,1,0:T(8,128)(2,1)}, u32[]{:S(2)}) copy-start(bf16[65,16,128]{2,1,0:T(8,128)(2,1)} %get-tuple-element.27) | copy-start | bytes 798724
  21.0 54.4 %copy-start.4 = (bf16[65,16,128]{2,1,0:T(8,128)(2,1)S(1)}, bf16[65,16,128]{2,1,0:T(8,128)(2,1)}, u32[]{:S(2)}) copy-start(bf16[65,16,128]{2,1,0:T(8,128)(2,1)} %get-tuple-element.28) | copy-start | bytes 798724
  21.0 57.2 %copy-start.3 = (bf16[65,16,128]{2,1,0:T(8,128)(2,1)S(1)}, bf16[65,16,128]{2,1,0:T(8,128)(2,1)}, u32[]{:S(2)}) copy-start(bf16[65,16,128]{2,1,0:T(8,128)(2,1)} %get-tuple-element.29) | copy-start | bytes 798724
  21.0 57.2 %copy-start.2 = (bf16[65,16,128]{2,1,0:T(8,128)(2,1)S(1)}, bf16[65,16,128]{2,1,0:T(8,128)(2,1)}, u32[]{:S(2)}) copy-start(bf16[65,16,128]{2,1,0:T(8,128)(2,1)} %get-tuple-element.30) | copy-start | bytes 798724
  29.5 20.5 %collective-permute-start = (bf16[32,16,128]{2,1,0:T(8,128)(2,1)}, bf16[32,16,128]{2,1,0:T(8,128)(2,1)}, u32[]{:S(2)}, u32[]{:S(2)}) collective-permute-start(bf16[32,16,128]{2,1,0:T(8,128)(2,1)} %get-tuple-element.18), channel_id=1, source_target_pairs={{0,8},{1,9},{2,10},{3,11},{4,12},{5,13},{6,14},{7,15},{8,0},{9,1},... | collective-permute-start | bytes 393224 | tf_op jit(solution)/shard_map/ppermute | solution.py:342
  31.9 21.7 %collective-permute-start.1 = (bf16[32,16,128]{2,1,0:T(8,128)(2,1)}, bf16[32,16,128]{2,1,0:T(8,128)(2,1)}, u32[]{:S(2)}, u32[]{:S(2)}) collective-permute-start(bf16[32,16,128]{2,1,0:T(8,128)(2,1)} %get-tuple-element.19), channel_id=1, source_target_pairs={{0,9},{1,8},{2,11},{3,10},{4,13},{5,12},{6,15},{7,14},{8,1},{9,0},... | collective-permute-start | bytes 393224 | tf_op jit(solution)/shard_map/ppermute | solution.py:342
  32.4 43.0 %collective-permute-start.4 = (bf16[33,16,128]{2,1,0:T(8,128)(2,1)}, bf16[33,16,128]{2,1,0:T(8,128)(2,1)}, u32[]{:S(2)}, u32[]{:S(2)}) collective-permute-start(bf16[33,16,128]{2,1,0:T(8,128)(2,1)} %get-tuple-element.23), channel_id=1, source_target_pairs={{0,8},{1,9},{2,10},{3,11},{4,12},{5,13},{6,14},{7,15},{8,0},{9,1},... | collective-permute-start | bytes 405512 | tf_op jit(solution)/shard_map/ppermute | solution.py:342
  34.8 43.4 %collective-permute-start.5 = (bf16[33,16,128]{2,1,0:T(8,128)(2,1)}, bf16[33,16,128]{2,1,0:T(8,128)(2,1)}, u32[]{:S(2)}, u32[]{:S(2)}) collective-permute-start(bf16[33,16,128]{2,1,0:T(8,128)(2,1)} %get-tuple-element.24), channel_id=1, source_target_pairs={{0,9},{1,8},{2,11},{3,10},{4,13},{5,12},{6,15},{7,14},{8,1},{9,0},... | collective-permute-start | bytes 405512 | tf_op jit(solution)/shard_map/ppermute | solution.py:342
  35.1 43.1 %collective-permute-start.6 = (bf16[33,16,128]{2,1,0:T(8,128)(2,1)}, bf16[33,16,128]{2,1,0:T(8,128)(2,1)}, u32[]{:S(2)}, u32[]{:S(2)}) collective-permute-start(bf16[33,16,128]{2,1,0:T(8,128)(2,1)} %get-tuple-element.25), channel_id=1, source_target_pairs={{0,10},{1,11},{2,8},{3,9},{4,14},{5,15},{6,12},{7,13},{8,2},{9,3},... | collective-permute-start | bytes 405512 | tf_op jit(solution)/shard_map/ppermute | solution.py:342
  50.0 19.0 %collective-permute-start.2 = (bf16[32,16,128]{2,1,0:T(8,128)(2,1)}, bf16[32,16,128]{2,1,0:T(8,128)(2,1)S(1)}, u32[]{:S(2)}, u32[]{:S(2)}) collective-permute-start(bf16[32,16,128]{2,1,0:T(8,128)(2,1)} %get-tuple-element.20), channel_id=1, source_target_pairs={{0,10},{1,11},{2,8},{3,9},{4,14},{5,15},{6,12},{7,13},{8,2},{9,3},... | collective-permute-start | bytes 393224 | tf_op jit(solution)/shard_map/ppermute | solution.py:342
  53.5 21.2 %collective-permute-start.3 = (bf16[32,16,128]{2,1,0:T(8,128)(2,1)}, bf16[32,16,128]{2,1,0:T(8,128)(2,1)S(1)}, u32[]{:S(2)}, u32[]{:S(2)}) collective-permute-start(bf16[32,16,128]{2,1,0:T(8,128)(2,1)} %get-tuple-element.21), channel_id=1, source_target_pairs={{0,11},{1,10},{2,9},{3,8},{4,15},{5,14},{6,13},{7,12},{8,3},{9,2},... | collective-permute-start | bytes 393224 | tf_op jit(solution)/shard_map/ppermute | solution.py:342
  69.0 5.8 %copy-start.10 = (bf16[32,16,128]{2,1,0:T(8,128)(2,1)}, bf16[32,16,128]{2,1,0:T(8,128)(2,1)S(1)}, u32[]{:S(2)}) copy-start(bf16[32,16,128]{2,1,0:T(8,128)(2,1)S(1)} %collective-permute-done.2.rest_2_) | copy-start | bytes 393220
  69.0 32.4 %collective-permute-start.7 = (bf16[33,16,128]{2,1,0:T(8,128)(2,1)}, bf16[33,16,128]{2,1,0:T(8,128)(2,1)S(1)}, u32[]{:S(2)}, u32[]{:S(2)}) collective-permute-start(bf16[33,16,128]{2,1,0:T(8,128)(2,1)} %get-tuple-element.26), channel_id=1, source_target_pairs={{0,11},{1,10},{2,9},{3,8},{4,15},{5,14},{6,13},{7,12},{8,3},{9,2},... | collective-permute-start | bytes 405512 | tf_op jit(solution)/shard_map/ppermute | solution.py:342
  74.7 0.7 copy-start.11
  75.4 33.6 %collective-permute-start.8 = (bf16[65,16,128]{2,1,0:T(8,128)(2,1)S(1)}, bf16[65,16,128]{2,1,0:T(8,128)(2,1)S(1)}, u32[]{:S(2)}, u32[]{:S(2)}) collective-permute-start(bf16[65,16,128]{2,1,0:T(8,128)(2,1)S(1)} %copy-done.5), channel_id=1, source_target_pairs={{0,12},{1,13},{2,14},{3,15},{4,8},{5,9},{6,10},{7,11},{8,4},{9,5},... | collective-permute-start | bytes 798728 | tf_op jit(solution)/shard_map/ppermute | solution.py:342
  75.4 39.3 %collective-permute-start.9 = (bf16[65,16,128]{2,1,0:T(8,128)(2,1)S(1)}, bf16[65,16,128]{2,1,0:T(8,128)(2,1)S(1)}, u32[]{:S(2)}, u32[]{:S(2)}) collective-permute-start(bf16[65,16,128]{2,1,0:T(8,128)(2,1)S(1)} %copy-done.4), channel_id=1, source_target_pairs={{0,13},{1,12},{2,15},{3,14},{4,9},{5,8},{6,11},{7,10},{8,5},{9,4},... | collective-permute-start | bytes 798728 | tf_op jit(solution)/shard_map/ppermute | solution.py:342
  78.2 42.8 %collective-permute-start.10 = (bf16[65,16,128]{2,1,0:T(8,128)(2,1)S(1)}, bf16[65,16,128]{2,1,0:T(8,128)(2,1)S(1)}, u32[]{:S(2)}, u32[]{:S(2)}) collective-permute-start(bf16[65,16,128]{2,1,0:T(8,128)(2,1)S(1)} %copy-done.3), channel_id=1, source_target_pairs={{0,14},{1,15},{2,12},{3,13},{4,10},{5,11},{6,8},{7,9},{8,6},{9,7},... | collective-permute-start | bytes 798728 | tf_op jit(solution)/shard_map/ppermute | solution.py:342
  78.2 48.6 %collective-permute-start.11 = (bf16[65,16,128]{2,1,0:T(8,128)(2,1)S(1)}, bf16[65,16,128]{2,1,0:T(8,128)(2,1)}, u32[]{:S(2)}, u32[]{:S(2)}) collective-permute-start(bf16[65,16,128]{2,1,0:T(8,128)(2,1)S(1)} %copy-done.2), channel_id=1, source_target_pairs={{0,15},{1,14},{2,13},{3,12},{4,11},{5,10},{6,9},{7,8},{8,7},{9,6},... | collective-permute-start | bytes 798728 | tf_op jit(solution)/shard_map/ppermute | solution.py:342
  101.3 19.6 %copy-start.9 = (bf16[33,16,128]{2,1,0:T(8,128)(2,1)}, bf16[33,16,128]{2,1,0:T(8,128)(2,1)S(1)}, u32[]{:S(2)}) copy-start(bf16[33,16,128]{2,1,0:T(8,128)(2,1)S(1)} %collective-permute-done.7.rest_8_) | copy-start | bytes 405508
  109.0 17.8 %copy-start.6 = (bf16[65,16,128]{2,1,0:T(8,128)(2,1)}, bf16[65,16,128]{2,1,0:T(8,128)(2,1)S(1)}, u32[]{:S(2)}) copy-start(bf16[65,16,128]{2,1,0:T(8,128)(2,1)S(1)} %collective-permute-done.8.rest_9_) | copy-start | bytes 798724
  114.7 6.3 %copy-start.7 = (bf16[65,16,128]{2,1,0:T(8,128)(2,1)}, bf16[65,16,128]{2,1,0:T(8,128)(2,1)S(1)}, u32[]{:S(2)}) copy-start(bf16[65,16,128]{2,1,0:T(8,128)(2,1)S(1)} %collective-permute-done.9.rest_10_) | copy-start | bytes 798724
  121.0 0.7 copy-start.8
  126.8 1.4 copy-start

commit v2 on v1

--- a/solution.py
+++ b/solution.py
@@ -56,7 +56,7 @@
 
 def forward_kernel(*rest, near, subset, starts, count, extra):
     if extra:
-        meta_ref, *rest = rest
+        meta_ref, _, *rest = rest
     sub_hbm, taper_ref, first_hbm, second_ref, *rest = rest
     number = near + len(subset)
     outs = rest[: len(subset) + (1 if near else 0)]
@@ -167,7 +167,7 @@
         copy.wait()
 
 
-def forward(subgrid, taper, first, second, near, subset, starts, meta=None):
+def forward(subgrid, taper, first, second, near, subset, starts, meta=None, after=None):
     number, count, extra = near + len(subset), first.shape[1], 0 if meta is None else 1
     shapes = [jax.ShapeDtypeStruct((near, count + extra, 16, 128), bf16)] * (1 if near else 0)
     shapes += [jax.ShapeDtypeStruct((count - start + extra, 16, 128), bf16) for start in starts]
@@ -177,7 +177,7 @@
             forward_kernel, near=near, subset=subset, starts=starts, count=count, extra=extra
         ),
         grid=(1,),
-        in_specs=[pl.BlockSpec(memory_space=pltpu.SMEM)] * extra
+        in_specs=[pl.BlockSpec(memory_space=pltpu.SMEM), hbm][: 2 * extra]
         + [
             hbm,
             pl.BlockSpec((64, 128), lambda i: (0, 0)),
@@ -200,7 +200,7 @@
         compiler_params=pltpu.CompilerParams(vmem_limit_bytes=58 * MIB),
         cost_estimate=pl.CostEstimate(flops=160000000 * count, bytes_accessed=12 * MIB, transcendentals=0),
         name=f"forward{number}",
-    )(*([meta] * extra), subgrid, taper, first, second)
+    )(*([meta, after] if extra else []), subgrid, taper, first, second)
 
 
 def placing_matrix(tiles):
@@ -240,7 +240,7 @@
         in_specs=[whole(correction.shape), whole(table.shape)],
         out_specs=whole(shape.shape),
         out_shape=shape,
-        compiler_params=pltpu.CompilerParams(vmem_limit_bytes=58 * MIB, dimension_semantics=("arbitrary",)),
+        compiler_params=pltpu.CompilerParams(vmem_limit_bytes=24 * MIB, dimension_semantics=("arbitrary",)),
         cost_estimate=pl.CostEstimate(flops=6000000000, bytes_accessed=16 * MIB, transcendentals=0),
         name="scale",
     )(correction, table)
@@ -327,7 +327,7 @@
             pltpu.SemaphoreType.DMA((4,)),
             pltpu.SemaphoreType.DMA((2, 2)),
         ],
-        compiler_params=pltpu.CompilerParams(vmem_limit_bytes=58 * MIB),
+        compiler_params=pltpu.CompilerParams(vmem_limit_bytes=34 * MIB),
         cost_estimate=pl.CostEstimate(flops=8000000000, bytes_accessed=16 * MIB, transcendentals=0),
         name="final",
     )(scaled, *pieces)
@@ -348,7 +348,7 @@
     early = forward(*inputs, first[:, :32], second, 0, EARLY, (0,) * len(EARLY))
     starts = tuple(32 if s in EARLY else 0 for s in FAR)
     meta = jnp.concatenate([counts, positions, channels])
-    near, *far = forward(*inputs, first, second, NEAR, FAR, starts, meta)
+    near, *far = forward(*inputs, first, second, NEAR, FAR, starts, meta, early[-1])
     early = [exchange(piece, s) for s, piece in zip(EARLY, early)]
     far = [exchange(piece, s) for s, piece in zip(FAR, far)]
     halves = [list(range(NEAR)), list(range(NEAR, 2 * NEAR))]

time: 139 us -> 154 us (1.11)
  local copies, waits for them, and re-layouts: 3.43 us -> 15.8 us
  waiting for transfers between devices: 70.5 us -> 73.7 us
  Pallas kernels: 37.6 us -> 35.5 us
    unnamed x24 -> x40, local copies, waits for them, and re-layouts: 2.74 us -> 15.8 us
    pallas_call x1, Pallas kernels: 5.68 us -> 1.52 us  [scale(): pl.pallas_call(scale_kernel, grid=(1,), in_specs=[whole(correction.shape)...]
    ppermute x12, waiting for transfers between devices: 70.5 us -> 73.7 us  [exchange(): return lax.ppermute(piece, 'facet', [(i, i ^ s) for i in range(16)])]
    pallas_call x1, Pallas kernels: 9.62 us -> 11.7 us  [final(): pl.pallas_call(functools.partial(final_kernel, early=len(early), far=len(...]
  transfers between devices with their start and end apart: 13 -> 13, of which waited for: 8 -> 8; matrix products, arithmetic and copies ran while one was open for 0% -> 0% of each run, Pallas kernels for 10% -> 1%
where the time goes in v2:
time: 154 us; the launch traced here: 153 us
  waiting for transfers between devices  73.7 us (48%)
  Pallas kernels  35.5 us (23%)
  starting transfers between devices  24.9 us (16%)
  local copies, waits for them, and re-layouts  15.8 us (10%)
  between operations  2.2 us (1%)
    ppermute x12, waiting for transfers between devices, exchange(): return lax.ppermute(piece, 'facet', [(i, i ^ s) for i in range(16)])  73.7 us
    pallas_call x2, Pallas kernels, forward(): pl.pallas_call(functools.partial(forward_kernel, near=near, subset=subset...  22.2 us
    ppermute x12, starting transfers between devices, exchange(): return lax.ppermute(piece, 'facet', [(i, i ^ s) for i in range(16)])  20.2 us
    unnamed x40, local copies, waits for them, and re-layouts  15.8 us
    pallas_call x1, Pallas kernels, final(): pl.pallas_call(functools.partial(final_kernel, early=len(early), far=len(...  11.7 us
    all_to_all x1, starting transfers between devices, local(): lax.all_to_all(near, 'facet', split_axis=0, concat_axis=0, axis_index_gro...  4.66 us
  transfers between devices with their start and end apart: 13, of which 8 were waited for; matrix products, arithmetic and copies ran while one was open for 0% of the time, Pallas kernels for 1%

profile of v2, /device:TPU:13, one launch (start us, length us, event | category | flops | bytes accessed | tf_op | source)
XLA Modules:
  0.0 152.7 jit_solution(7104233150827959588)
XLA Ops:
  1.9 0.6 pad_add_fusion.rest_0_
  2.5 8.4 %forward4.1 = (bf16[32,16,128]{2,1,0:T(8,128)(2,1)}, bf16[32,16,128]{2,1,0:T(8,128)(2,1)}, bf16[32,16,128]{2,1,0:T(8,128)(2,1)}, bf16[32,16,128]{2,1,0:T(8,128)(2,1)}) custom-call(bf16[2,8192,128]{2,1,0:T(8,128)(2,1)} %bitcast.3, f32[64,128]{1,0:T(8,128)} %bitcast.5, f32[128,32,128]{2,1,0:T(8,128)} %constant.8.clone.rest_2_, ...), custom_call_target="tpu_custom_call" | custom-call | flops 5120000000 | bytes 12582912 | tf_op jit(solution)/shard_map/forward4/pallas_call | solution.py:175
  10.9 13.8 %forward16.1 = (bf16[8,65,16,128]{3,2,1,0:T(8,128)(2,1)}, bf16[33,16,128]{2,1,0:T(8,128)(2,1)}, bf16[33,16,128]{2,1,0:T(8,128)(2,1)}, bf16[33,16,128]{2,1,0:T(8,...) custom-call(s32[3]{0:T(128)} %pad_add_fusion.rest_0_, ...), custom_call_target="tpu_custom_call" | custom-call | flops 10240000000 | bytes 12582912 | tf_op jit(solution)/shard_map/forward16/pallas_call | solution.py:175
  24.8 0.0 copy-start.17
  24.8 0.0 copy-start.15
  24.9 4.7 %all-to-all-start = ((bf16[8,65,16,128]{3,2,1,0:T(8,128)(2,1)}), bf16[8,65,16,128]{3,2,1,0:T(8,128)(2,1)S(1)}, u32[]{:S(2)}, u32[]{:S(2)}) async-start(bf16[8,65,16,128]{3,2,1,0:T(8,128)(2,1)} %get-tuple-element.22), calls=%async_computation | async-start | bytes 4259840 | tf_op jit(solution)/shard_map/all_to_all | solution.py:355
  29.5 2.3 %collective-permute-start = (bf16[32,16,128]{2,1,0:T(8,128)(2,1)}, bf16[32,16,128]{2,1,0:T(8,128)(2,1)S(1)}, u32[]{:S(2)}, u32[]{:S(2)}) collective-permute-start(bf16[32,16,128]{2,1,0:T(8,128)(2,1)} %get-tuple-element.18), channel_id=1, source_target_pairs={{0,8},{1,9},{2,10},{3,11},{4,12},{5,13},{6,14},{7,15},{8,0},{9,1},... | collective-permute-start | bytes 393224 | tf_op jit(solution)/shard_map/ppermute | solution.py:342
  31.8 0.6 collective-permute-start.1
  32.4 2.3 %collective-permute-start.4 = (bf16[33,16,128]{2,1,0:T(8,128)(2,1)S(1)}, bf16[33,16,128]{2,1,0:T(8,128)(2,1)S(1)}, u32[]{:S(2)}, u32[]{:S(2)}) collective-permute-start(bf16[33,16,128]{2,1,0:T(8,128)(2,1)S(1)} %copy-done.17), channel_id=1, source_target_pairs={{0,8},{1,9},{2,10},{3,11},{4,12},{5,13},{6,14},{7,15},{8,0},{9,1},... | collective-permute-start | bytes 405512 | tf_op jit(solution)/shard_map/ppermute | solution.py:342
  34.7 0.3 collective-permute-start.5
  35.0 2.1 %collective-permute-start.6 = (bf16[33,16,128]{2,1,0:T(8,128)(2,1)}, bf16[33,16,128]{2,1,0:T(8,128)(2,1)S(1)}, u32[]{:S(2)}, u32[]{:S(2)}) collective-permute-start(bf16[33,16,128]{2,1,0:T(8,128)(2,1)} %get-tuple-element.25), channel_id=1, source_target_pairs={{0,10},{1,11},{2,8},{3,9},{4,14},{5,15},{6,12},{7,13},{8,2},{9,3},... | collective-permute-start | bytes 405512 | tf_op jit(solution)/shard_map/ppermute | solution.py:342
  37.1 21.3 %collective-permute-done.rest_0_ = bf16[32,16,128]{2,1,0:T(8,128)(2,1)S(1)} collective-permute-done((bf16[32,16,128]{2,1,0:T(8,128)(2,1)}, bf16[32,16,128]{2,1,0:T(8,128)(2,1)S(1)}, u32[]{:S(2)}, u32[]{:S(2)}) %collective-permute-start) | collective-permute-done | bytes 131104 | tf_op jit(solution)/shard_map/ppermute | solution.py:342
  58.4 0.7 copy-done.4
  59.1 0.0 collective-permute-start.2
  59.1 2.9 %collective-permute-done.1.rest_1_ = bf16[32,16,128]{2,1,0:T(8,128)(2,1)S(1)} collective-permute-done((bf16[32,16,128]{2,1,0:T(8,128)(2,1)}, bf16[32,16,128]{2,1,0:T(8,128)(2,1)S(1)}, u32[]{:S(2)}, u32[]{:S(2)}) %collective-permute-start.1) | collective-permute-done | bytes 131104 | tf_op jit(solution)/shard_map/ppermute | solution.py:342
  62.0 0.6 copy-done.6
  62.6 1.9 %collective-permute-start.3 = (bf16[32,16,128]{2,1,0:T(8,128)(2,1)S(1)}, bf16[32,16,128]{2,1,0:T(8,128)(2,1)S(1)}, u32[]{:S(2)}, u32[]{:S(2)}) collective-permute-start(bf16[32,16,128]{2,1,0:T(8,128)(2,1)S(1)} %copy-done.18), channel_id=1, source_target_pairs={{0,11},{1,10},{2,9},{3,8},{4,15},{5,14},{6,13},{7,12},{8,3},{9,2},... | collective-permute-start | bytes 393224 | tf_op jit(solution)/shard_map/ppermute | solution.py:342
  64.5 0.1 reshape.9.correction_ref
  64.6 11.1 %collective-permute-done.2.rest_2_ = bf16[32,16,128]{2,1,0:T(8,128)(2,1)S(1)} collective-permute-done((bf16[32,16,128]{2,1,0:T(8,128)(2,1)S(1)}, bf16[32,16,128]{2,1,0:T(8,128)(2,1)S(1)}, u32[]{:S(2)}, u32[]{:S(2)}) %collective-permute-start.2) | collective-permute-done | bytes 131104 | tf_op jit(solution)/shard_map/ppermute | solution.py:342
  75.7 0.6 copy-done.8
  76.3 4.5 %collective-permute-start.7 = (bf16[33,16,128]{2,1,0:T(8,128)(2,1)}, bf16[33,16,128]{2,1,0:T(8,128)(2,1)S(1)}, u32[]{:S(2)}, u32[]{:S(2)}) collective-permute-start(bf16[33,16,128]{2,1,0:T(8,128)(2,1)} %get-tuple-element.26), channel_id=1, source_target_pairs={{0,11},{1,10},{2,9},{3,8},{4,15},{5,14},{6,13},{7,12},{8,3},{9,2},... | collective-permute-start | bytes 405512 | tf_op jit(solution)/shard_map/ppermute | solution.py:342
  80.8 0.0 collective-permute-done.3.rest_3_
  80.8 0.7 copy-done.10
  81.5 2.8 %collective-permute-start.8 = (bf16[65,16,128]{2,1,0:T(8,128)(2,1)}, bf16[65,16,128]{2,1,0:T(8,128)(2,1)S(1)}, u32[]{:S(2)}, u32[]{:S(2)}) collective-permute-start(bf16[65,16,128]{2,1,0:T(8,128)(2,1)} %get-tuple-element.27), channel_id=1, source_target_pairs={{0,12},{1,13},{2,14},{3,15},{4,8},{5,9},{6,10},{7,11},{8,4},{9,5},... | collective-permute-start | bytes 798728 | tf_op jit(solution)/shard_map/ppermute | solution.py:342
  84.2 0.0 collective-permute-done.4.rest_5_
  84.2 0.6 collective-permute-start.9
  84.8 0.0 collective-permute-done.5.rest_6_
  84.8 0.6 collective-permute-start.10
  85.3 0.7 copy-done
  86.0 2.4 %collective-permute-start.11 = (bf16[65,16,128]{2,1,0:T(8,128)(2,1)}, bf16[65,16,128]{2,1,0:T(8,128)(2,1)S(1)}, u32[]{:S(2)}, u32[]{:S(2)}) collective-permute-start(bf16[65,16,128]{2,1,0:T(8,128)(2,1)} %get-tuple-element.30), channel_id=1, source_target_pairs={{0,15},{1,14},{2,13},{3,12},{4,11},{5,10},{6,9},{7,8},{8,7},{9,6},... | collective-permute-start | bytes 798728 | tf_op jit(solution)/shard_map/ppermute | solution.py:342
  88.4 2.2 %copy-done.12 = f32[64,128,128]{2,1,0:T(8,128)S(1)} copy-done((f32[64,128,128]{2,1,0:T(8,128)S(1)}, f32[64,128,128]{2,1,0:T(8,128)}, u32[]{:S(2)}) %copy-start.12) | copy-done | bytes 4194328
  90.6 1.5 scale.1.scaled_hbm
  92.1 0.0 copy-start.13
  92.1 2.0 %copy-done.13 = bf16[64,128,256]{2,1,0:T(8,128)(2,1)} copy-done((bf16[64,128,256]{2,1,0:T(8,128)(2,1)}, bf16[64,128,256]{2,1,0:T(8,128)(2,1)S(1)}, u32[]{:S(2)}) %copy-start.13) | copy-done | bytes 4194328
  94.1 15.6 %collective-permute-done.7.rest_8_ = bf16[33,16,128]{2,1,0:T(8,128)(2,1)S(1)} collective-permute-done((bf16[33,16,128]{2,1,0:T(8,128)(2,1)}, bf16[33,16,128]{2,1,0:T(8,128)(2,1)S(1)}, u32[]{:S(2)}, u32[]{:S(2)}) %collective-permute-start.7) | collective-permute-done | bytes 135200 | tf_op jit(solution)/shard_map/ppermute | solution.py:342
  109.7 0.7 copy-done.2
  110.4 5.5 %collective-permute-done.8.rest_9_ = bf16[65,16,128]{2,1,0:T(8,128)(2,1)S(1)} collective-permute-done((bf16[65,16,128]{2,1,0:T(8,128)(2,1)}, bf16[65,16,128]{2,1,0:T(8,128)(2,1)S(1)}, u32[]{:S(2)}, u32[]{:S(2)}) %collective-permute-start.8) | collective-permute-done | bytes 266272 | tf_op jit(solution)/shard_map/ppermute | solution.py:342
  115.9 5.7 %collective-permute-done.9.rest_10_ = bf16[65,16,128]{2,1,0:T(8,128)(2,1)S(1)} collective-permute-done((bf16[65,16,128]{2,1,0:T(8,128)(2,1)}, bf16[65,16,128]{2,1,0:T(8,128)(2,1)S(1)}, u32[]{:S(2)}, u32[]{:S(2)}) %collective-permute-start.9) | collective-permute-done | bytes 266272 | tf_op jit(solution)/shard_map/ppermute | solution.py:342
  121.6 5.9 %collective-permute-done.10.rest_11_ = bf16[65,16,128]{2,1,0:T(8,128)(2,1)S(1)} collective-permute-done((bf16[65,16,128]{2,1,0:T(8,128)(2,1)}, bf16[65,16,128]{2,1,0:T(8,128)(2,1)S(1)}, u32[]{:S(2)}, u32[]{:S(2)}) %collective-permute-start.10) | collective-permute-done | bytes 266272 | tf_op jit(solution)/shard_map/ppermute | solution.py:342
  127.5 5.7 %collective-permute-done.11.rest_12_ = bf16[65,16,128]{2,1,0:T(8,128)(2,1)S(1)} collective-permute-done((bf16[65,16,128]{2,1,0:T(8,128)(2,1)}, bf16[65,16,128]{2,1,0:T(8,128)(2,1)S(1)}, u32[]{:S(2)}, u32[]{:S(2)}) %collective-permute-start.11) | collective-permute-done | bytes 266272 | tf_op jit(solution)/shard_map/ppermute | solution.py:342
  133.2 0.9 copy-done.1
  134.1 0.9 copy-done.3
  135.0 0.9 copy-done.5
  135.9 0.9 copy-done.7
  136.8 0.9 copy-done.9
  137.7 0.9 copy-done.11
  138.7 2.2 %copy-done.14 = bf16[64,128,256]{2,1,0:T(8,128)(2,1)S(1)} copy-done((bf16[64,128,256]{2,1,0:T(8,128)(2,1)S(1)}, bf16[64,128,256]{2,1,0:T(8,128)(2,1)}, u32[]{:S(2)}) %copy-start.14) | copy-done | bytes 4194328
  140.8 11.7 %final.1 = f32[2,2,64,64,128]{4,3,2,1,0:T(8,128)} custom-call(bf16[64,128,256]{2,1,0:T(8,128)(2,1)S(1)} %copy-done.14, bf16[32,16,128]{2,1,0:T(8,128)(2,1)S(1)} %copy-done.5, bf16[32,16,128]{2,1,0:T(8,128)(2,1)S(1)} %copy-done.7, bf16[32,16,128]{2,1,0:T(8,128)(2,1)S(1)} %copy-done.9, bf16[32,16,128]{2,1,0:T(8,128)(2,1)S(1)} %copy-done.11, ...), custom_call_target="tpu_custom_call" | custom-call | flops 8000000000 | bytes 16777216 | tf_op jit(solution)/shard_map/final/pallas_call | solution.py:316
  (24 shorter events, 0.0 us)
Async XLA Ops:
  24.8 7.6 %copy-start.17 = (bf16[33,16,128]{2,1,0:T(8,128)(2,1)S(1)}, bf16[33,16,128]{2,1,0:T(8,128)(2,1)}, u32[]{:S(2)}) copy-start(bf16[33,16,128]{2,1,0:T(8,128)(2,1)} %get-tuple-element.23) | copy-start | bytes 405508
  24.8 9.9 %copy-start.16 = (bf16[33,16,128]{2,1,0:T(8,128)(2,1)S(1)}, bf16[33,16,128]{2,1,0:T(8,128)(2,1)}, u32[]{:S(2)}) copy-start(bf16[33,16,128]{2,1,0:T(8,128)(2,1)} %get-tuple-element.24) | copy-start | bytes 405508
  24.8 34.3 %copy-start.19 = (bf16[32,16,128]{2,1,0:T(8,128)(2,1)S(1)}, bf16[32,16,128]{2,1,0:T(8,128)(2,1)}, u32[]{:S(2)}) copy-start(bf16[32,16,128]{2,1,0:T(8,128)(2,1)} %get-tuple-element.20) | copy-start | bytes 393220
  24.8 37.8 %copy-start.18 = (bf16[32,16,128]{2,1,0:T(8,128)(2,1)S(1)}, bf16[32,16,128]{2,1,0:T(8,128)(2,1)}, u32[]{:S(2)}) copy-start(bf16[32,16,128]{2,1,0:T(8,128)(2,1)} %get-tuple-element.21.rest_1_) | copy-start | bytes 393220
  24.8 39.7 %copy-start.15 = (f32[4096]{0:T(1024)S(1)}, f32[4096]{0:T(1024)}, u32[]{:S(2)}) copy-start(f32[4096]{0:T(1024)} %param.15) | copy-start | bytes 49156
  24.9 108.4 %all-to-all-start = ((bf16[8,65,16,128]{3,2,1,0:T(8,128)(2,1)}), bf16[8,65,16,128]{3,2,1,0:T(8,128)(2,1)S(1)}, u32[]{:S(2)}, u32[]{:S(2)}) async-start(bf16[8,65,16,128]{3,2,1,0:T(8,128)(2,1)} %get-tuple-element.22), calls=%async_computation | async-start | bytes 4259840 | tf_op jit(solution)/shard_map/all_to_all | solution.py:355
  29.5 28.9 %collective-permute-start = (bf16[32,16,128]{2,1,0:T(8,128)(2,1)}, bf16[32,16,128]{2,1,0:T(8,128)(2,1)S(1)}, u32[]{:S(2)}, u32[]{:S(2)}) collective-permute-start(bf16[32,16,128]{2,1,0:T(8,128)(2,1)} %get-tuple-element.18), channel_id=1, source_target_pairs={{0,8},{1,9},{2,10},{3,11},{4,12},{5,13},{6,14},{7,15},{8,0},{9,1},... | collective-permute-start | bytes 393224 | tf_op jit(solution)/shard_map/ppermute | solution.py:342
  31.8 30.2 %collective-permute-start.1 = (bf16[32,16,128]{2,1,0:T(8,128)(2,1)}, bf16[32,16,128]{2,1,0:T(8,128)(2,1)S(1)}, u32[]{:S(2)}, u32[]{:S(2)}) collective-permute-start(bf16[32,16,128]{2,1,0:T(8,128)(2,1)} %get-tuple-element.19), channel_id=1, source_target_pairs={{0,9},{1,8},{2,11},{3,10},{4,13},{5,12},{6,15},{7,14},{8,1},{9,0},... | collective-permute-start | bytes 393224 | tf_op jit(solution)/shard_map/ppermute | solution.py:342
  32.4 51.8 %collective-permute-start.4 = (bf16[33,16,128]{2,1,0:T(8,128)(2,1)S(1)}, bf16[33,16,128]{2,1,0:T(8,128)(2,1)S(1)}, u32[]{:S(2)}, u32[]{:S(2)}) collective-permute-start(bf16[33,16,128]{2,1,0:T(8,128)(2,1)S(1)} %copy-done.17), channel_id=1, source_target_pairs={{0,8},{1,9},{2,10},{3,11},{4,12},{5,13},{6,14},{7,15},{8,0},{9,1},... | collective-permute-start | bytes 405512 | tf_op jit(solution)/shard_map/ppermute | solution.py:342
  34.7 50.1 %collective-permute-start.5 = (bf16[33,16,128]{2,1,0:T(8,128)(2,1)S(1)}, bf16[33,16,128]{2,1,0:T(8,128)(2,1)S(1)}, u32[]{:S(2)}, u32[]{:S(2)}) collective-permute-start(bf16[33,16,128]{2,1,0:T(8,128)(2,1)S(1)} %copy-done.16), channel_id=1, source_target_pairs={{0,9},{1,8},{2,11},{3,10},{4,13},{5,12},{6,15},{7,14},{8,1},{9,0},... | collective-permute-start | bytes 405512 | tf_op jit(solution)/shard_map/ppermute | solution.py:342
  35.0 50.3 %collective-permute-start.6 = (bf16[33,16,128]{2,1,0:T(8,128)(2,1)}, bf16[33,16,128]{2,1,0:T(8,128)(2,1)S(1)}, u32[]{:S(2)}, u32[]{:S(2)}) collective-permute-start(bf16[33,16,128]{2,1,0:T(8,128)(2,1)} %get-tuple-element.25), channel_id=1, source_target_pairs={{0,10},{1,11},{2,8},{3,9},{4,14},{5,15},{6,12},{7,13},{8,2},{9,3},... | collective-permute-start | bytes 405512 | tf_op jit(solution)/shard_map/ppermute | solution.py:342
  58.4 0.7 copy-start.4
  59.1 16.6 %collective-permute-start.2 = (bf16[32,16,128]{2,1,0:T(8,128)(2,1)S(1)}, bf16[32,16,128]{2,1,0:T(8,128)(2,1)S(1)}, u32[]{:S(2)}, u32[]{:S(2)}) collective-permute-start(bf16[32,16,128]{2,1,0:T(8,128)(2,1)S(1)} %copy-done.19), channel_id=1, source_target_pairs={{0,10},{1,11},{2,8},{3,9},{4,14},{5,15},{6,12},{7,13},{8,2},{9,3},... | collective-permute-start | bytes 393224 | tf_op jit(solution)/shard_map/ppermute | solution.py:342
  62.0 0.7 copy-start.6
  62.6 18.2 %collective-permute-start.3 = (bf16[32,16,128]{2,1,0:T(8,128)(2,1)S(1)}, bf16[32,16,128]{2,1,0:T(8,128)(2,1)S(1)}, u32[]{:S(2)}, u32[]{:S(2)}) collective-permute-start(bf16[32,16,128]{2,1,0:T(8,128)(2,1)S(1)} %copy-done.18), channel_id=1, source_target_pairs={{0,11},{1,10},{2,9},{3,8},{4,15},{5,14},{6,13},{7,12},{8,3},{9,2},... | collective-permute-start | bytes 393224 | tf_op jit(solution)/shard_map/ppermute | solution.py:342
  75.7 0.6 copy-start.8
  76.3 33.4 %collective-permute-start.7 = (bf16[33,16,128]{2,1,0:T(8,128)(2,1)}, bf16[33,16,128]{2,1,0:T(8,128)(2,1)S(1)}, u32[]{:S(2)}, u32[]{:S(2)}) collective-permute-start(bf16[33,16,128]{2,1,0:T(8,128)(2,1)} %get-tuple-element.26), channel_id=1, source_target_pairs={{0,11},{1,10},{2,9},{3,8},{4,15},{5,14},{6,13},{7,12},{8,3},{9,2},... | collective-permute-start | bytes 405512 | tf_op jit(solution)/shard_map/ppermute | solution.py:342
  80.8 0.7 copy-start.10
  81.5 34.4 %collective-permute-start.8 = (bf16[65,16,128]{2,1,0:T(8,128)(2,1)}, bf16[65,16,128]{2,1,0:T(8,128)(2,1)S(1)}, u32[]{:S(2)}, u32[]{:S(2)}) collective-permute-start(bf16[65,16,128]{2,1,0:T(8,128)(2,1)} %get-tuple-element.27), channel_id=1, source_target_pairs={{0,12},{1,13},{2,14},{3,15},{4,8},{5,9},{6,10},{7,11},{8,4},{9,5},... | collective-permute-start | bytes 798728 | tf_op jit(solution)/shard_map/ppermute | solution.py:342
  84.2 37.4 %collective-permute-start.9 = (bf16[65,16,128]{2,1,0:T(8,128)(2,1)}, bf16[65,16,128]{2,1,0:T(8,128)(2,1)S(1)}, u32[]{:S(2)}, u32[]{:S(2)}) collective-permute-start(bf16[65,16,128]{2,1,0:T(8,128)(2,1)} %get-tuple-element.28), channel_id=1, source_target_pairs={{0,13},{1,12},{2,15},{3,14},{4,9},{5,8},{6,11},{7,10},{8,5},{9,4},... | collective-permute-start | bytes 798728 | tf_op jit(solution)/shard_map/ppermute | solution.py:342
  84.8 42.7 %collective-permute-start.10 = (bf16[65,16,128]{2,1,0:T(8,128)(2,1)}, bf16[65,16,128]{2,1,0:T(8,128)(2,1)S(1)}, u32[]{:S(2)}, u32[]{:S(2)}) collective-permute-start(bf16[65,16,128]{2,1,0:T(8,128)(2,1)} %get-tuple-element.29), channel_id=1, source_target_pairs={{0,14},{1,15},{2,12},{3,13},{4,10},{5,11},{6,8},{7,9},{8,6},{9,7},... | collective-permute-start | bytes 798728 | tf_op jit(solution)/shard_map/ppermute | solution.py:342
  85.3 0.7 copy-start
  86.0 47.2 %collective-permute-start.11 = (bf16[65,16,128]{2,1,0:T(8,128)(2,1)}, bf16[65,16,128]{2,1,0:T(8,128)(2,1)S(1)}, u32[]{:S(2)}, u32[]{:S(2)}) collective-permute-start(bf16[65,16,128]{2,1,0:T(8,128)(2,1)} %get-tuple-element.30), channel_id=1, source_target_pairs={{0,15},{1,14},{2,13},{3,12},{4,11},{5,10},{6,9},{7,8},{8,7},{9,6},... | collective-permute-start | bytes 798728 | tf_op jit(solution)/shard_map/ppermute | solution.py:342
  88.4 2.2 %copy-start.12 = (f32[64,128,128]{2,1,0:T(8,128)S(1)}, f32[64,128,128]{2,1,0:T(8,128)}, u32[]{:S(2)}) copy-start(f32[64,128,128]{2,1,0:T(8,128)} %constant.11.clone.table_ref) | copy-start | bytes 12582916
  92.1 2.0 %copy-start.13 = (bf16[64,128,256]{2,1,0:T(8,128)(2,1)}, bf16[64,128,256]{2,1,0:T(8,128)(2,1)S(1)}, u32[]{:S(2)}) copy-start(bf16[64,128,256]{2,1,0:T(8,128)(2,1)S(1)} %scale.1.scaled_hbm) | copy-start | bytes 12582916
  109.7 0.7 copy-start.2
  133.2 0.9 copy-start.1
  134.1 0.9 copy-start.3
  135.0 0.9 copy-start.5
  135.9 0.9 copy-start.7
  136.8 0.9 copy-start.9
  137.7 0.9 copy-start.11
  138.7 2.2 %copy-start.14 = (bf16[64,128,256]{2,1,0:T(8,128)(2,1)S(1)}, bf16[64,128,256]{2,1,0:T(8,128)(2,1)}, u32[]{:S(2)}) copy-start(bf16[64,128,256]{2,1,0:T(8,128)(2,1)} %copy-done.13) | copy-start | bytes 12582916

commit v3 on v0

--- a/solution.py
+++ b/solution.py
@@ -320,8 +320,8 @@
     )(scaled, *pieces)
 
 
-EARLY = (8, 9, 10)
-LATE = (8, 9, 10, 3, 11, 2, 12, 1, 4, 13, 5, 6, 14, 7, 15)
+EARLY = (8, 9, 10, 11)
+LATE = (8, 9, 10, 11, 4, 12, 3, 5, 13, 2, 6, 14, 7, 15, 1)
 
 
 def exchange(piece, s):

time: 131 us -> 117 us (0.89)
  the two profiles are of different devices: /device:TPU:1 before, /device:TPU:13 now
where the time goes in v3:
time: 117 us
  starting transfers between devices  41.7 us (36%)
  Pallas kernels  38.2 us (33%)
  waiting for transfers between devices  32.8 us (28%)
  between operations  2.33 us (2%)
  local copies, waits for them, and re-layouts  1.52 us (1%)
    ppermute x19, starting transfers between devices, exchange(): return lax.ppermute(piece, 'facet', [(i, i ^ s) for i in range(16)])  41.7 us
    ppermute x19, waiting for transfers between devices, exchange(): return lax.ppermute(piece, 'facet', [(i, i ^ s) for i in range(16)])  32.8 us
    pallas_call x2, Pallas kernels, forward(): pl.pallas_call(functools.partial(forward_kernel, subset=subset, starts=st...  22.6 us
    pallas_call x1, Pallas kernels, final(): pl.pallas_call(functools.partial(final_kernel, sizes=sizes), in_specs=[hb...  9.91 us
    pallas_call x1, Pallas kernels, scale(): pl.pallas_call(scale_kernel, grid=(1,), in_specs=[whole(correction.shape)...  5.71 us
  transfers between devices with their start and end apart: 19, of which 6 were waited for; matrix products, arithmetic and copies ran while one was open for 1% of the time, Pallas kernels for 17%

profile of v3, /device:TPU:13, one launch (start us, length us, event | category | flops | bytes accessed | tf_op | source)
XLA Modules:
  0.0 117.1 jit_solution(9649221049910164274)
XLA Ops:
  0.0 8.4 %forward4.1 = (bf16[32,16,128]{2,1,0:T(8,128)(2,1)}, bf16[32,16,128]{2,1,0:T(8,128)(2,1)}, bf16[32,16,128]{2,1,0:T(8,128)(2,1)}, bf16[32,16,128]{2,1,0:T(8,128)(2,1)}) custom-call(bf16[2,8192,128]{2,1,0:T(8,128)(2,1)} %bitcast.3, f32[64,128]{1,0:T(8,128)} %bitcast.5, f32[128,32,128]{2,1,0:T(8,128)} %constant.8.clone.rest_2_, ...), custom_call_target="tpu_custom_call" | custom-call | flops 5120000000 | bytes 12582912 | tf_op jit(solution)/shard_map/forward4/pallas_call | solution.py:165
  8.4 2.4 %collective-permute-start = (bf16[32,16,128]{2,1,0:T(8,128)(2,1)}, bf16[32,16,128]{2,1,0:T(8,128)(2,1)S(1)}, u32[]{:S(2)}, u32[]{:S(2)}) collective-permute-start(bf16[32,16,128]{2,1,0:T(8,128)(2,1)} %get-tuple-element.25), channel_id=1, source_target_pairs={{0,8},{1,9},{2,10},{3,11},{4,12},{5,13},{6,14},{7,15},{8,0},{9,1},... | collective-permute-start | bytes 393224 | tf_op jit(solution)/shard_map/ppermute | solution.py:328
  10.8 0.9 collective-permute-start.1
  11.7 2.3 %collective-permute-start.2 = (bf16[32,16,128]{2,1,0:T(8,128)(2,1)}, bf16[32,16,128]{2,1,0:T(8,128)(2,1)S(1)}, u32[]{:S(2)}, u32[]{:S(2)}) collective-permute-start(bf16[32,16,128]{2,1,0:T(8,128)(2,1)} %get-tuple-element.27), channel_id=1, source_target_pairs={{0,10},{1,11},{2,8},{3,9},{4,14},{5,15},{6,12},{7,13},{8,2},{9,3},... | collective-permute-start | bytes 393224 | tf_op jit(solution)/shard_map/ppermute | solution.py:328
  13.9 1.2 %collective-permute-start.3 = (bf16[32,16,128]{2,1,0:T(8,128)(2,1)}, bf16[32,16,128]{2,1,0:T(8,128)(2,1)S(1)}, u32[]{:S(2)}, u32[]{:S(2)}) collective-permute-start(bf16[32,16,128]{2,1,0:T(8,128)(2,1)} %get-tuple-element.28), channel_id=1, source_target_pairs={{0,11},{1,10},{2,9},{3,8},{4,15},{5,14},{6,13},{7,12},{8,3},{9,2},... | collective-permute-start | bytes 393224 | tf_op jit(solution)/shard_map/ppermute | solution.py:328
  17.1 0.6 pad_add_fusion.rest_0_
  17.7 14.2 %forward16.1 = (bf16[33,16,128]{2,1,0:T(8,128)(2,1)}, bf16[33,16,128]{2,1,0:T(8,128)(2,1)}, bf16[33,16,128]{2,1,0:T(8,128)(2,1)}, bf16[33,16,128]{2,1,0:T(8,128)...) custom-call(s32[3]{0:T(128)} %pad_add_fusion.rest_0_, ...), custom_call_target="tpu_custom_call" | custom-call | flops 10240000000 | bytes 12582912 | tf_op jit(solution)/shard_map/forward16/pallas_call | solution.py:165
  31.9 0.2 collective-permute-start.8
  32.1 0.0 collective-permute-done.rest_0_
  32.1 1.8 %collective-permute-start.4 = (bf16[33,16,128]{2,1,0:T(8,128)(2,1)}, bf16[33,16,128]{2,1,0:T(8,128)(2,1)S(1)}, u32[]{:S(2)}, u32[]{:S(2)}) collective-permute-start(bf16[33,16,128]{2,1,0:T(8,128)(2,1)} %get-tuple-element.29), channel_id=1, source_target_pairs={{0,8},{1,9},{2,10},{3,11},{4,12},{5,13},{6,14},{7,15},{8,0},{9,1},... | collective-permute-start | bytes 405512 | tf_op jit(solution)/shard_map/ppermute | solution.py:328
  33.9 0.0 collective-permute-done.1.rest_1_
  34.0 1.2 %collective-permute-start.5 = (bf16[33,16,128]{2,1,0:T(8,128)(2,1)}, bf16[33,16,128]{2,1,0:T(8,128)(2,1)S(1)}, u32[]{:S(2)}, u32[]{:S(2)}) collective-permute-start(bf16[33,16,128]{2,1,0:T(8,128)(2,1)} %get-tuple-element.30), channel_id=1, source_target_pairs={{0,9},{1,8},{2,11},{3,10},{4,13},{5,12},{6,15},{7,14},{8,1},{9,0},... | collective-permute-start | bytes 405512 | tf_op jit(solution)/shard_map/ppermute | solution.py:328
  35.1 0.0 collective-permute-done.2.rest_2_
  35.1 2.3 %collective-permute-start.6 = (bf16[33,16,128]{2,1,0:T(8,128)(2,1)}, bf16[33,16,128]{2,1,0:T(8,128)(2,1)S(1)}, u32[]{:S(2)}, u32[]{:S(2)}) collective-permute-start(bf16[33,16,128]{2,1,0:T(8,128)(2,1)} %get-tuple-element.31), channel_id=1, source_target_pairs={{0,10},{1,11},{2,8},{3,9},{4,14},{5,15},{6,12},{7,13},{8,2},{9,3},... | collective-permute-start | bytes 405512 | tf_op jit(solution)/shard_map/ppermute | solution.py:328
  37.4 0.0 collective-permute-done.3.rest_3_
  37.4 1.3 %collective-permute-start.7 = (bf16[33,16,128]{2,1,0:T(8,128)(2,1)}, bf16[33,16,128]{2,1,0:T(8,128)(2,1)S(1)}, u32[]{:S(2)}, u32[]{:S(2)}) collective-permute-start(bf16[33,16,128]{2,1,0:T(8,128)(2,1)} %get-tuple-element.32), channel_id=1, source_target_pairs={{0,11},{1,10},{2,9},{3,8},{4,15},{5,14},{6,13},{7,12},{8,3},{9,2},... | collective-permute-start | bytes 405512 | tf_op jit(solution)/shard_map/ppermute | solution.py:328
  38.7 4.1 %collective-permute-done.4.rest_4_ = bf16[33,16,128]{2,1,0:T(8,128)(2,1)S(1)} collective-permute-done((bf16[33,16,128]{2,1,0:T(8,128)(2,1)}, bf16[33,16,128]{2,1,0:T(8,128)(2,1)S(1)}, u32[]{:S(2)}, u32[]{:S(2)}) %collective-permute-start.4) | collective-permute-done | bytes 135200 | tf_op jit(solution)/shard_map/ppermute | solution.py:328
  42.9 1.3 %collective-permute-start.9 = (bf16[65,16,128]{2,1,0:T(8,128)(2,1)}, bf16[65,16,128]{2,1,0:T(8,128)(2,1)S(1)}, u32[]{:S(2)}, u32[]{:S(2)}) collective-permute-start(bf16[65,16,128]{2,1,0:T(8,128)(2,1)} %get-tuple-element.34), channel_id=1, source_target_pairs={{0,12},{1,13},{2,14},{3,15},{4,8},{5,9},{6,10},{7,11},{8,4},{9,5},... | collective-permute-start | bytes 798728 | tf_op jit(solution)/shard_map/ppermute | solution.py:328
  44.2 3.9 %collective-permute-done.5.rest_5_ = bf16[33,16,128]{2,1,0:T(8,128)(2,1)S(1)} collective-permute-done((bf16[33,16,128]{2,1,0:T(8,128)(2,1)}, bf16[33,16,128]{2,1,0:T(8,128)(2,1)S(1)}, u32[]{:S(2)}, u32[]{:S(2)}) %collective-permute-start.5) | collective-permute-done | bytes 135200 | tf_op jit(solution)/shard_map/ppermute | solution.py:328
  48.1 11.8 %collective-permute-start.10 = (bf16[65,16,128]{2,1,0:T(8,128)(2,1)}, bf16[65,16,128]{2,1,0:T(8,128)(2,1)S(1)}, u32[]{:S(2)}, u32[]{:S(2)}) collective-permute-start(bf16[65,16,128]{2,1,0:T(8,128)(2,1)} %get-tuple-element.35), channel_id=1, source_target_pairs={{0,3},{1,2},{2,1},{3,0},{4,7},{5,6},{6,5},{7,4},{8,11},{9,10},{10,... | collective-permute-start | bytes 798728 | tf_op jit(solution)/shard_map/ppermute | solution.py:328
  59.8 0.0 collective-permute-done.6.rest_6_
  59.8 3.6 %collective-permute-start.11 = (bf16[65,16,128]{2,1,0:T(8,128)(2,1)}, bf16[65,16,128]{2,1,0:T(8,128)(2,1)S(1)}, u32[]{:S(2)}, u32[]{:S(2)}) collective-permute-start(bf16[65,16,128]{2,1,0:T(8,128)(2,1)} %get-tuple-element.36), channel_id=1, source_target_pairs={{0,5},{1,4},{2,7},{3,6},{4,1},{5,0},{6,3},{7,2},{8,13},{9,12},{10,... | collective-permute-start | bytes 798728 | tf_op jit(solution)/shard_map/ppermute | solution.py:328
  63.5 0.0 collective-permute-done.7.rest_7_
  63.5 1.2 collective-permute-start.12
  64.6 0.0 collective-permute-done.8.rest_8_
  64.6 0.2 collective-permute-start.13
  64.9 0.0 copy-done
  64.9 0.7 reshape.9.correction_ref
  65.6 10.8 %collective-permute-done.9.rest_9_ = bf16[65,16,128]{2,1,0:T(8,128)(2,1)S(1)} collective-permute-done((bf16[65,16,128]{2,1,0:T(8,128)(2,1)}, bf16[65,16,128]{2,1,0:T(8,128)(2,1)S(1)}, u32[]{:S(2)}, u32[]{:S(2)}) %collective-permute-start.9) | collective-permute-done | bytes 266272 | tf_op jit(solution)/shard_map/ppermute | solution.py:328
  76.4 0.0 collective-permute-start.14
  76.4 0.0 collective-permute-done.10.rest_10_
  76.4 0.1 collective-permute-start.15
  76.5 0.0 collective-permute-done.11.rest_11_
  76.5 6.2 %collective-permute-start.16 = (bf16[65,16,128]{2,1,0:T(8,128)(2,1)}, bf16[65,16,128]{2,1,0:T(8,128)(2,1)S(1)}, u32[]{:S(2)}, u32[]{:S(2)}) collective-permute-start(bf16[65,16,128]{2,1,0:T(8,128)(2,1)} %get-tuple-element.41), channel_id=1, source_target_pairs={{0,7},{1,6},{2,5},{3,4},{4,3},{5,2},{6,1},{7,0},{8,15},{9,14},{10,... | collective-permute-start | bytes 798728 | tf_op jit(solution)/shard_map/ppermute | solution.py:328
  82.7 0.0 collective-permute-done.12.rest_12_
  82.7 0.0 collective-permute-start.17
  82.7 0.0 collective-permute-done.13.rest_13_
  82.7 0.0 copy-start.6
  82.7 3.8 %collective-permute-start.18 = (bf16[65,16,128]{2,1,0:T(8,128)(2,1)}, bf16[65,16,128]{2,1,0:T(8,128)(2,1)S(1)}, u32[]{:S(2)}, u32[]{:S(2)}) collective-permute-start(bf16[65,16,128]{2,1,0:T(8,128)(2,1)} %get-tuple-element.43), channel_id=1, source_target_pairs={{0,1},{1,0},{2,3},{3,2},{4,5},{5,4},{6,7},{7,6},{8,9},{9,8},{10,11... | collective-permute-start | bytes 798728 | tf_op jit(solution)/shard_map/ppermute | solution.py:328
  86.5 5.7 %scale.1.scaled_hbm = bf16[64,128,256]{2,1,0:T(8,128)(2,1)} custom-call(f32[64,64]{1,0:T(8,128)} %reshape.9.correction_ref, f32[64,128,128]{2,1,0:T(8,128)} %constant.11.clone.table_ref), custom_call_target="tpu_custom_call" | custom-call | flops 6000000000 | bytes 16777216 | tf_op jit(solution)/shard_map/scale/pallas_call | solution.py:225
  92.3 0.0 collective-permute-done.14.rest_14_
  92.4 0.5 collective-permute-done.15.rest_15_
  92.9 7.0 %collective-permute-done.16.rest_16_ = bf16[65,16,128]{2,1,0:T(8,128)(2,1)S(1)} collective-permute-done((bf16[65,16,128]{2,1,0:T(8,128)(2,1)}, bf16[65,16,128]{2,1,0:T(8,128)(2,1)S(1)}, u32[]{:S(2)}, u32[]{:S(2)}) %collective-permute-start.16) | collective-permute-done | bytes 266272 | tf_op jit(solution)/shard_map/ppermute | solution.py:328
  99.9 6.4 %collective-permute-done.17.rest_17_ = bf16[65,16,128]{2,1,0:T(8,128)(2,1)S(1)} collective-permute-done((bf16[65,16,128]{2,1,0:T(8,128)(2,1)}, bf16[65,16,128]{2,1,0:T(8,128)(2,1)S(1)}, u32[]{:S(2)}, u32[]{:S(2)}) %collective-permute-start.17) | collective-permute-done | bytes 266272 | tf_op jit(solution)/shard_map/ppermute | solution.py:328
  106.2 0.0 collective-permute-done.18.rest_18_
  106.3 0.7 copy-done.10
  107.0 0.1 copy-done.11
  107.0 9.9 %final.1 = f32[2,2,64,64,128]{4,3,2,1,0:T(8,128)} custom-call(bf16[64,128,256]{2,1,0:T(8,128)(2,1)} %scale.1.scaled_hbm, bf16[32,16,128]{2,1,0:T(8,128)(2,1)} %copy-done.16, bf16[32,16,128]{2,1,0:T(8,128)(2,1)} %copy-done.17, bf16[32,16,128]{2,1,0:T(8,128)(2,1)} %copy-done.18, bf16[32,16,128]{2,1,0:T(8,128)(2,1)} %copy-done.19, ...), custom_call_target="tpu_custom_call" | custom-call | flops 8000000000 | bytes 16777216 | tf_op jit(solution)/shard_map/final/pallas_call | solution.py:303
  (36 shorter events, 0.1 us)
Async XLA Ops:
  8.4 23.7 %collective-permute-start = (bf16[32,16,128]{2,1,0:T(8,128)(2,1)}, bf16[32,16,128]{2,1,0:T(8,128)(2,1)S(1)}, u32[]{:S(2)}, u32[]{:S(2)}) collective-permute-start(bf16[32,16,128]{2,1,0:T(8,128)(2,1)} %get-tuple-element.25), channel_id=1, source_target_pairs={{0,8},{1,9},{2,10},{3,11},{4,12},{5,13},{6,14},{7,15},{8,0},{9,1},... | collective-permute-start | bytes 393224 | tf_op jit(solution)/shard_map/ppermute | solution.py:328
  10.8 23.2 %collective-permute-start.1 = (bf16[32,16,128]{2,1,0:T(8,128)(2,1)}, bf16[32,16,128]{2,1,0:T(8,128)(2,1)S(1)}, u32[]{:S(2)}, u32[]{:S(2)}) collective-permute-start(bf16[32,16,128]{2,1,0:T(8,128)(2,1)} %get-tuple-element.26), channel_id=1, source_target_pairs={{0,9},{1,8},{2,11},{3,10},{4,13},{5,12},{6,15},{7,14},{8,1},{9,0},... | collective-permute-start | bytes 393224 | tf_op jit(solution)/shard_map/ppermute | solution.py:328
  11.7 23.5 %collective-permute-start.2 = (bf16[32,16,128]{2,1,0:T(8,128)(2,1)}, bf16[32,16,128]{2,1,0:T(8,128)(2,1)S(1)}, u32[]{:S(2)}, u32[]{:S(2)}) collective-permute-start(bf16[32,16,128]{2,1,0:T(8,128)(2,1)} %get-tuple-element.27), channel_id=1, source_target_pairs={{0,10},{1,11},{2,8},{3,9},{4,14},{5,15},{6,12},{7,13},{8,2},{9,3},... | collective-permute-start | bytes 393224 | tf_op jit(solution)/shard_map/ppermute | solution.py:328
  13.9 23.5 %collective-permute-start.3 = (bf16[32,16,128]{2,1,0:T(8,128)(2,1)}, bf16[32,16,128]{2,1,0:T(8,128)(2,1)S(1)}, u32[]{:S(2)}, u32[]{:S(2)}) collective-permute-start(bf16[32,16,128]{2,1,0:T(8,128)(2,1)} %get-tuple-element.28), channel_id=1, source_target_pairs={{0,11},{1,10},{2,9},{3,8},{4,15},{5,14},{6,13},{7,12},{8,3},{9,2},... | collective-permute-start | bytes 393224 | tf_op jit(solution)/shard_map/ppermute | solution.py:328
  17.7 47.2 %copy-start = (f32[4096]{0:T(1024)S(1)}, f32[4096]{0:T(1024)}, u32[]{:S(2)}) copy-start(f32[4096]{0:T(1024)} %param.15) | copy-start | bytes 49156
  31.9 32.7 %collective-permute-start.8 = (bf16[65,16,128]{2,1,0:T(8,128)(2,1)}, bf16[65,16,128]{2,1,0:T(8,128)(2,1)S(1)}, u32[]{:S(2)}, u32[]{:S(2)}) collective-permute-start(bf16[65,16,128]{2,1,0:T(8,128)(2,1)} %get-tuple-element.33), channel_id=1, source_target_pairs={{0,4},{1,5},{2,6},{3,7},{4,0},{5,1},{6,2},{7,3},{8,12},{9,13},{10,... | collective-permute-start | bytes 798728 | tf_op jit(solution)/shard_map/ppermute | solution.py:328
  32.1 60.1 %copy-start.16 = (bf16[32,16,128]{2,1,0:T(8,128)(2,1)}, bf16[32,16,128]{2,1,0:T(8,128)(2,1)S(1)}, u32[]{:S(2)}) copy-start(bf16[32,16,128]{2,1,0:T(8,128)(2,1)S(1)} %collective-permute-done.rest_0_) | copy-start | bytes 393220
  32.1 10.7 %collective-permute-start.4 = (bf16[33,16,128]{2,1,0:T(8,128)(2,1)}, bf16[33,16,128]{2,1,0:T(8,128)(2,1)S(1)}, u32[]{:S(2)}, u32[]{:S(2)}) collective-permute-start(bf16[33,16,128]{2,1,0:T(8,128)(2,1)} %get-tuple-element.29), channel_id=1, source_target_pairs={{0,8},{1,9},{2,10},{3,11},{4,12},{5,13},{6,14},{7,15},{8,0},{9,1},... | collective-permute-start | bytes 405512 | tf_op jit(solution)/shard_map/ppermute | solution.py:328
  33.9 58.3 %copy-start.17 = (bf16[32,16,128]{2,1,0:T(8,128)(2,1)}, bf16[32,16,128]{2,1,0:T(8,128)(2,1)S(1)}, u32[]{:S(2)}) copy-start(bf16[32,16,128]{2,1,0:T(8,128)(2,1)S(1)} %collective-permute-done.1.rest_1_) | copy-start | bytes 393220
  34.0 14.1 %collective-permute-start.5 = (bf16[33,16,128]{2,1,0:T(8,128)(2,1)}, bf16[33,16,128]{2,1,0:T(8,128)(2,1)S(1)}, u32[]{:S(2)}, u32[]{:S(2)}) collective-permute-start(bf16[33,16,128]{2,1,0:T(8,128)(2,1)} %get-tuple-element.30), channel_id=1, source_target_pairs={{0,9},{1,8},{2,11},{3,10},{4,13},{5,12},{6,15},{7,14},{8,1},{9,0},... | collective-permute-start | bytes 405512 | tf_op jit(solution)/shard_map/ppermute | solution.py:328
  35.1 57.1 %copy-start.18 = (bf16[32,16,128]{2,1,0:T(8,128)(2,1)}, bf16[32,16,128]{2,1,0:T(8,128)(2,1)S(1)}, u32[]{:S(2)}) copy-start(bf16[32,16,128]{2,1,0:T(8,128)(2,1)S(1)} %collective-permute-done.2.rest_2_) | copy-start | bytes 393220
  35.1 24.7 %collective-permute-start.6 = (bf16[33,16,128]{2,1,0:T(8,128)(2,1)}, bf16[33,16,128]{2,1,0:T(8,128)(2,1)S(1)}, u32[]{:S(2)}, u32[]{:S(2)}) collective-permute-start(bf16[33,16,128]{2,1,0:T(8,128)(2,1)} %get-tuple-element.31), channel_id=1, source_target_pairs={{0,10},{1,11},{2,8},{3,9},{4,14},{5,15},{6,12},{7,13},{8,2},{9,3},... | collective-permute-start | bytes 405512 | tf_op jit(solution)/shard_map/ppermute | solution.py:328
  37.4 54.8 %copy-start.19 = (bf16[32,16,128]{2,1,0:T(8,128)(2,1)}, bf16[32,16,128]{2,1,0:T(8,128)(2,1)S(1)}, u32[]{:S(2)}) copy-start(bf16[32,16,128]{2,1,0:T(8,128)(2,1)S(1)} %collective-permute-done.3.rest_3_) | copy-start | bytes 393220
  37.4 26.1 %collective-permute-start.7 = (bf16[33,16,128]{2,1,0:T(8,128)(2,1)}, bf16[33,16,128]{2,1,0:T(8,128)(2,1)S(1)}, u32[]{:S(2)}, u32[]{:S(2)}) collective-permute-start(bf16[33,16,128]{2,1,0:T(8,128)(2,1)} %get-tuple-element.32), channel_id=1, source_target_pairs={{0,11},{1,10},{2,9},{3,8},{4,15},{5,14},{6,13},{7,12},{8,3},{9,2},... | collective-permute-start | bytes 405512 | tf_op jit(solution)/shard_map/ppermute | solution.py:328
  42.8 49.4 %copy-start.12 = (bf16[33,16,128]{2,1,0:T(8,128)(2,1)}, bf16[33,16,128]{2,1,0:T(8,128)(2,1)S(1)}, u32[]{:S(2)}) copy-start(bf16[33,16,128]{2,1,0:T(8,128)(2,1)S(1)} %collective-permute-done.4.rest_4_) | copy-start | bytes 405508
  42.9 33.5 %collective-permute-start.9 = (bf16[65,16,128]{2,1,0:T(8,128)(2,1)}, bf16[65,16,128]{2,1,0:T(8,128)(2,1)S(1)}, u32[]{:S(2)}, u32[]{:S(2)}) collective-permute-start(bf16[65,16,128]{2,1,0:T(8,128)(2,1)} %get-tuple-element.34), channel_id=1, source_target_pairs={{0,12},{1,13},{2,14},{3,15},{4,8},{5,9},{6,10},{7,11},{8,4},{9,5},... | collective-permute-start | bytes 798728 | tf_op jit(solution)/shard_map/ppermute | solution.py:328
  48.1 44.2 %copy-start.13 = (bf16[33,16,128]{2,1,0:T(8,128)(2,1)}, bf16[33,16,128]{2,1,0:T(8,128)(2,1)S(1)}, u32[]{:S(2)}) copy-start(bf16[33,16,128]{2,1,0:T(8,128)(2,1)S(1)} %collective-permute-done.5.rest_5_) | copy-start | bytes 405508
  48.1 28.3 %collective-permute-start.10 = (bf16[65,16,128]{2,1,0:T(8,128)(2,1)}, bf16[65,16,128]{2,1,0:T(8,128)(2,1)S(1)}, u32[]{:S(2)}, u32[]{:S(2)}) collective-permute-start(bf16[65,16,128]{2,1,0:T(8,128)(2,1)} %get-tuple-element.35), channel_id=1, source_target_pairs={{0,3},{1,2},{2,1},{3,0},{4,7},{5,6},{6,5},{7,4},{8,11},{9,10},{10,... | collective-permute-start | bytes 798728 | tf_op jit(solution)/shard_map/ppermute | solution.py:328
  59.8 32.4 %copy-start.14 = (bf16[33,16,128]{2,1,0:T(8,128)(2,1)}, bf16[33,16,128]{2,1,0:T(8,128)(2,1)S(1)}, u32[]{:S(2)}) copy-start(bf16[33,16,128]{2,1,0:T(8,128)(2,1)S(1)} %collective-permute-done.6.rest_6_) | copy-start | bytes 405508
  59.8 16.6 %collective-permute-start.11 = (bf16[65,16,128]{2,1,0:T(8,128)(2,1)}, bf16[65,16,128]{2,1,0:T(8,128)(2,1)S(1)}, u32[]{:S(2)}, u32[]{:S(2)}) collective-permute-start(bf16[65,16,128]{2,1,0:T(8,128)(2,1)} %get-tuple-element.36), channel_id=1, source_target_pairs={{0,5},{1,4},{2,7},{3,6},{4,1},{5,0},{6,3},{7,2},{8,13},{9,12},{10,... | collective-permute-start | bytes 798728 | tf_op jit(solution)/shard_map/ppermute | solution.py:328
  63.5 28.8 %copy-start.15 = (bf16[33,16,128]{2,1,0:T(8,128)(2,1)}, bf16[33,16,128]{2,1,0:T(8,128)(2,1)S(1)}, u32[]{:S(2)}) copy-start(bf16[33,16,128]{2,1,0:T(8,128)(2,1)S(1)} %collective-permute-done.7.rest_7_) | copy-start | bytes 405508
  63.5 19.2 %collective-permute-start.12 = (bf16[65,16,128]{2,1,0:T(8,128)(2,1)}, bf16[65,16,128]{2,1,0:T(8,128)(2,1)S(1)}, u32[]{:S(2)}, u32[]{:S(2)}) collective-permute-start(bf16[65,16,128]{2,1,0:T(8,128)(2,1)} %get-tuple-element.37), channel_id=1, source_target_pairs={{0,13},{1,12},{2,15},{3,14},{4,9},{5,8},{6,11},{7,10},{8,5},{9,4},... | collective-permute-start | bytes 798728 | tf_op jit(solution)/shard_map/ppermute | solution.py:328
  64.6 27.7 %copy-start.1 = (bf16[65,16,128]{2,1,0:T(8,128)(2,1)}, bf16[65,16,128]{2,1,0:T(8,128)(2,1)S(1)}, u32[]{:S(2)}) copy-start(bf16[65,16,128]{2,1,0:T(8,128)(2,1)S(1)} %collective-permute-done.8.rest_8_) | copy-start | bytes 798724
  64.6 18.1 %collective-permute-start.13 = (bf16[65,16,128]{2,1,0:T(8,128)(2,1)}, bf16[65,16,128]{2,1,0:T(8,128)(2,1)S(1)}, u32[]{:S(2)}, u32[]{:S(2)}) collective-permute-start(bf16[65,16,128]{2,1,0:T(8,128)(2,1)} %get-tuple-element.38), channel_id=1, source_target_pairs={{0,2},{1,3},{2,0},{3,1},{4,6},{5,7},{6,4},{7,5},{8,10},{9,11},{10,... | collective-permute-start | bytes 798728 | tf_op jit(solution)/shard_map/ppermute | solution.py:328
  76.4 15.9 %copy-start.2 = (bf16[65,16,128]{2,1,0:T(8,128)(2,1)}, bf16[65,16,128]{2,1,0:T(8,128)(2,1)S(1)}, u32[]{:S(2)}) copy-start(bf16[65,16,128]{2,1,0:T(8,128)(2,1)S(1)} %collective-permute-done.9.rest_9_) | copy-start | bytes 798724
  76.4 16.0 %collective-permute-start.14 = (bf16[65,16,128]{2,1,0:T(8,128)(2,1)}, bf16[65,16,128]{2,1,0:T(8,128)(2,1)S(1)}, u32[]{:S(2)}, u32[]{:S(2)}) collective-permute-start(bf16[65,16,128]{2,1,0:T(8,128)(2,1)} %get-tuple-element.39), channel_id=1, source_target_pairs={{0,6},{1,7},{2,4},{3,5},{4,2},{5,3},{6,0},{7,1},{8,14},{9,15},{10,... | collective-permute-start | bytes 798728 | tf_op jit(solution)/shard_map/ppermute | solution.py:328
  76.4 15.9 %copy-start.3 = (bf16[65,16,128]{2,1,0:T(8,128)(2,1)}, bf16[65,16,128]{2,1,0:T(8,128)(2,1)S(1)}, u32[]{:S(2)}) copy-start(bf16[65,16,128]{2,1,0:T(8,128)(2,1)S(1)} %collective-permute-done.10.rest_10_) | copy-start | bytes 798724
  76.4 16.5 %collective-permute-start.15 = (bf16[65,16,128]{2,1,0:T(8,128)(2,1)}, bf16[65,16,128]{2,1,0:T(8,128)(2,1)S(1)}, u32[]{:S(2)}, u32[]{:S(2)}) collective-permute-start(bf16[65,16,128]{2,1,0:T(8,128)(2,1)} %get-tuple-element.40), channel_id=1, source_target_pairs={{0,14},{1,15},{2,12},{3,13},{4,10},{5,11},{6,8},{7,9},{8,6},{9,7},... | collective-permute-start | bytes 798728 | tf_op jit(solution)/shard_map/ppermute | solution.py:328
  76.5 15.8 %copy-start.4 = (bf16[65,16,128]{2,1,0:T(8,128)(2,1)}, bf16[65,16,128]{2,1,0:T(8,128)(2,1)S(1)}, u32[]{:S(2)}) copy-start(bf16[65,16,128]{2,1,0:T(8,128)(2,1)S(1)} %collective-permute-done.11.rest_11_) | copy-start | bytes 798724
  76.5 23.4 %collective-permute-start.16 = (bf16[65,16,128]{2,1,0:T(8,128)(2,1)}, bf16[65,16,128]{2,1,0:T(8,128)(2,1)S(1)}, u32[]{:S(2)}, u32[]{:S(2)}) collective-permute-start(bf16[65,16,128]{2,1,0:T(8,128)(2,1)} %get-tuple-element.41), channel_id=1, source_target_pairs={{0,7},{1,6},{2,5},{3,4},{4,3},{5,2},{6,1},{7,0},{8,15},{9,14},{10,... | collective-permute-start | bytes 798728 | tf_op jit(solution)/shard_map/ppermute | solution.py:328
  82.7 9.6 %copy-start.5 = (bf16[65,16,128]{2,1,0:T(8,128)(2,1)}, bf16[65,16,128]{2,1,0:T(8,128)(2,1)S(1)}, u32[]{:S(2)}) copy-start(bf16[65,16,128]{2,1,0:T(8,128)(2,1)S(1)} %collective-permute-done.12.rest_12_) | copy-start | bytes 798724
  82.7 23.5 %collective-permute-start.17 = (bf16[65,16,128]{2,1,0:T(8,128)(2,1)}, bf16[65,16,128]{2,1,0:T(8,128)(2,1)S(1)}, u32[]{:S(2)}, u32[]{:S(2)}) collective-permute-start(bf16[65,16,128]{2,1,0:T(8,128)(2,1)} %get-tuple-element.42), channel_id=1, source_target_pairs={{0,15},{1,14},{2,13},{3,12},{4,11},{5,10},{6,9},{7,8},{8,7},{9,6},... | collective-permute-start | bytes 798728 | tf_op jit(solution)/shard_map/ppermute | solution.py:328
  82.7 9.6 %copy-start.6 = (bf16[65,16,128]{2,1,0:T(8,128)(2,1)}, bf16[65,16,128]{2,1,0:T(8,128)(2,1)S(1)}, u32[]{:S(2)}) copy-start(bf16[65,16,128]{2,1,0:T(8,128)(2,1)S(1)} %collective-permute-done.13.rest_13_) | copy-start | bytes 798724
  82.7 23.5 %collective-permute-start.18 = (bf16[65,16,128]{2,1,0:T(8,128)(2,1)}, bf16[65,16,128]{2,1,0:T(8,128)(2,1)S(1)}, u32[]{:S(2)}, u32[]{:S(2)}) collective-permute-start(bf16[65,16,128]{2,1,0:T(8,128)(2,1)} %get-tuple-element.43), channel_id=1, source_target_pairs={{0,1},{1,0},{2,3},{3,2},{4,5},{5,4},{6,7},{7,6},{8,9},{9,8},{10,11... | collective-permute-start | bytes 798728 | tf_op jit(solution)/shard_map/ppermute | solution.py:328
  92.3 13.9 %copy-start.7 = (bf16[65,16,128]{2,1,0:T(8,128)(2,1)}, bf16[65,16,128]{2,1,0:T(8,128)(2,1)S(1)}, u32[]{:S(2)}) copy-start(bf16[65,16,128]{2,1,0:T(8,128)(2,1)S(1)} %collective-permute-done.14.rest_14_) | copy-start | bytes 798724
  92.9 13.4 %copy-start.8 = (bf16[65,16,128]{2,1,0:T(8,128)(2,1)}, bf16[65,16,128]{2,1,0:T(8,128)(2,1)S(1)}, u32[]{:S(2)}) copy-start(bf16[65,16,128]{2,1,0:T(8,128)(2,1)S(1)} %collective-permute-done.15.rest_15_) | copy-start | bytes 798724
  99.9 6.4 %copy-start.9 = (bf16[65,16,128]{2,1,0:T(8,128)(2,1)}, bf16[65,16,128]{2,1,0:T(8,128)(2,1)S(1)}, u32[]{:S(2)}) copy-start(bf16[65,16,128]{2,1,0:T(8,128)(2,1)S(1)} %collective-permute-done.16.rest_16_) | copy-start | bytes 798724
  106.2 0.7 copy-start.10
  106.2 0.8 copy-start.11

commit v4 on v3

--- a/solution.py
+++ b/solution.py
@@ -57,10 +57,12 @@
 def forward_kernel(*rest, subset, starts, count, extra):
     if extra:
         meta_ref, *rest = rest
-    sub_hbm, taper_ref, first_hbm, second_ref, *rest = rest
+    sub_hbm, taper_hbm, first_hbm, second_hbm, *rest = rest
     outs = rest[: len(subset)]
-    sub_ref, first_ref, plain, tapers, mid, pieces, sub_sem, first_sem, out_sem = rest[len(subset) :]
+    sub_ref, taper_ref, first_ref, second_ref, plain, tapers, mid, pieces, sub_sem, first_sem, out_sem = rest[len(subset) :]
     sub_copies, first_copies, out_copies = [], [], []
+    taper_copy = pltpu.make_async_copy(taper_hbm, taper_ref, first_sem.at[4])
+    taper_copy.start()
     for q in range(4):
         for x in range(2):
             rows = pl.ds(q * 2048, 2048)
@@ -72,6 +74,9 @@
         copy = pltpu.make_async_copy(first_hbm.at[rows], first_ref.at[rows], first_sem.at[q])
         copy.start()
         first_copies.append(copy)
+    second_copy = pltpu.make_async_copy(second_hbm, second_ref, first_sem.at[5])
+    second_copy.start()
+    taper_copy.wait()
     turned = taper_ref[...].T
     tapers[:, 0:64] = turned
     tapers[:, 64:128] = turned
@@ -116,6 +121,7 @@
                 mid[pl.ds(b, count, stride=PITCH_MID), :] = mine[:count]
                 mid[pl.ds(128 + b, count, stride=PITCH_MID), :] = mine[count:]
 
+    second_copy.wait()
     me = lax.axis_index("facet")
     blocks = [pl.ds(pl.multiple_of((me ^ s) * 16, 16), 16) for s in subset]
     high = jnp.concatenate([second_ref[rows, 0:256] for rows in blocks], axis=0)
@@ -168,21 +174,23 @@
         in_specs=[pl.BlockSpec(memory_space=pltpu.SMEM)] * extra
         + [
             hbm,
-            pl.BlockSpec((64, 128), lambda i: (0, 0)),
             hbm,
-            pl.BlockSpec((256, 512), lambda i: (0, 0)),
+            hbm,
+            hbm,
         ],
         out_specs=[hbm] * number,
         out_shape=shapes,
         scratch_shapes=[
             pltpu.VMEM((2, 8192, 128), bf16),
+            pltpu.VMEM((64, 128), f32),
             pltpu.VMEM((128, count, 128), f32),
+            pltpu.VMEM((256, 512), bf16),
             pltpu.VMEM((128 * PITCH, 128), f32),
             pltpu.VMEM((128, 128), f32),
             pltpu.VMEM((count * PITCH_MID, 128), f32),
             pltpu.VMEM((number, count + extra, 16, 128), bf16),
             pltpu.SemaphoreType.DMA((4, 2)),
-            pltpu.SemaphoreType.DMA((4,)),
+            pltpu.SemaphoreType.DMA((6,)),
             pltpu.SemaphoreType.DMA((2, number)),
         ],
         compiler_params=pltpu.CompilerParams(vmem_limit_bytes=58 * MIB),

time: 117 us -> 117 us (level)
  no operation moved by 1% of the time
where the time goes in v4:
time: 117 us; the launch traced here: 116 us
  starting transfers between devices  41.7 us (36%)
  Pallas kernels  37.6 us (32%)
  waiting for transfers between devices  32.7 us (28%)
  between operations  2.33 us (2%)
  local copies, waits for them, and re-layouts  1.52 us (1%)
    ppermute x19, starting transfers between devices, exchange(): return lax.ppermute(piece, 'facet', [(i, i ^ s) for i in range(16)])  41.7 us
    ppermute x19, waiting for transfers between devices, exchange(): return lax.ppermute(piece, 'facet', [(i, i ^ s) for i in range(16)])  32.7 us
    pallas_call x2, Pallas kernels, forward(): pl.pallas_call(functools.partial(forward_kernel, subset=subset, starts=st...  21.9 us
    pallas_call x1, Pallas kernels, final(): pl.pallas_call(functools.partial(final_kernel, sizes=sizes), in_specs=[hb...  9.91 us
    pallas_call x1, Pallas kernels, scale(): pl.pallas_call(scale_kernel, grid=(1,), in_specs=[whole(correction.shape)...  5.71 us
  transfers between devices with their start and end apart: 19, of which 6 were waited for; matrix products, arithmetic and copies ran while one was open for 1% of the time, Pallas kernels for 17%

profile of v4, /device:TPU:13, one launch (start us, length us, event | category | flops | bytes accessed | tf_op | source)
XLA Modules:
  0.0 116.4 jit_solution(8216325869165541167)
XLA Ops:
  0.0 7.6 %forward4.1 = (bf16[32,16,128]{2,1,0:T(8,128)(2,1)}, bf16[32,16,128]{2,1,0:T(8,128)(2,1)}, bf16[32,16,128]{2,1,0:T(8,128)(2,1)}, bf16[32,16,128]{2,1,0:T(8,128)(2,1)}) custom-call(bf16[2,8192,128]{2,1,0:T(8,128)(2,1)} %bitcast.3, f32[64,128]{1,0:T(8,128)} %bitcast.5, f32[128,32,128]{2,1,0:T(8,128)} %constant.8.clone.rest_2_, ...), custom_call_target="tpu_custom_call" | custom-call | flops 5120000000 | bytes 12582912 | tf_op jit(solution)/shard_map/forward4/pallas_call | solution.py:171
  7.6 2.4 %collective-permute-start = (bf16[32,16,128]{2,1,0:T(8,128)(2,1)}, bf16[32,16,128]{2,1,0:T(8,128)(2,1)S(1)}, u32[]{:S(2)}, u32[]{:S(2)}) collective-permute-start(bf16[32,16,128]{2,1,0:T(8,128)(2,1)} %get-tuple-element.25), channel_id=1, source_target_pairs={{0,8},{1,9},{2,10},{3,11},{4,12},{5,13},{6,14},{7,15},{8,0},{9,1},... | collective-permute-start | bytes 393224 | tf_op jit(solution)/shard_map/ppermute | solution.py:336
  10.0 0.9 collective-permute-start.1
  10.9 2.3 %collective-permute-start.2 = (bf16[32,16,128]{2,1,0:T(8,128)(2,1)}, bf16[32,16,128]{2,1,0:T(8,128)(2,1)S(1)}, u32[]{:S(2)}, u32[]{:S(2)}) collective-permute-start(bf16[32,16,128]{2,1,0:T(8,128)(2,1)} %get-tuple-element.27), channel_id=1, source_target_pairs={{0,10},{1,11},{2,8},{3,9},{4,14},{5,15},{6,12},{7,13},{8,2},{9,3},... | collective-permute-start | bytes 393224 | tf_op jit(solution)/shard_map/ppermute | solution.py:336
  13.1 1.2 %collective-permute-start.3 = (bf16[32,16,128]{2,1,0:T(8,128)(2,1)}, bf16[32,16,128]{2,1,0:T(8,128)(2,1)S(1)}, u32[]{:S(2)}, u32[]{:S(2)}) collective-permute-start(bf16[32,16,128]{2,1,0:T(8,128)(2,1)} %get-tuple-element.28), channel_id=1, source_target_pairs={{0,11},{1,10},{2,9},{3,8},{4,15},{5,14},{6,13},{7,12},{8,3},{9,2},... | collective-permute-start | bytes 393224 | tf_op jit(solution)/shard_map/ppermute | solution.py:336
  16.3 0.6 pad_add_fusion.rest_0_
  16.9 14.3 %forward16.1 = (bf16[33,16,128]{2,1,0:T(8,128)(2,1)}, bf16[33,16,128]{2,1,0:T(8,128)(2,1)}, bf16[33,16,128]{2,1,0:T(8,128)(2,1)}, bf16[33,16,128]{2,1,0:T(8,128)...) custom-call(s32[3]{0:T(128)} %pad_add_fusion.rest_0_, ...), custom_call_target="tpu_custom_call" | custom-call | flops 10240000000 | bytes 12582912 | tf_op jit(solution)/shard_map/forward16/pallas_call | solution.py:171
  31.3 0.2 collective-permute-start.8
  31.5 0.0 collective-permute-done.rest_0_
  31.5 1.8 %collective-permute-start.4 = (bf16[33,16,128]{2,1,0:T(8,128)(2,1)}, bf16[33,16,128]{2,1,0:T(8,128)(2,1)S(1)}, u32[]{:S(2)}, u32[]{:S(2)}) collective-permute-start(bf16[33,16,128]{2,1,0:T(8,128)(2,1)} %get-tuple-element.29), channel_id=1, source_target_pairs={{0,8},{1,9},{2,10},{3,11},{4,12},{5,13},{6,14},{7,15},{8,0},{9,1},... | collective-permute-start | bytes 405512 | tf_op jit(solution)/shard_map/ppermute | solution.py:336
  33.3 0.0 collective-permute-done.1.rest_1_
  33.3 1.2 %collective-permute-start.5 = (bf16[33,16,128]{2,1,0:T(8,128)(2,1)}, bf16[33,16,128]{2,1,0:T(8,128)(2,1)S(1)}, u32[]{:S(2)}, u32[]{:S(2)}) collective-permute-start(bf16[33,16,128]{2,1,0:T(8,128)(2,1)} %get-tuple-element.30), channel_id=1, source_target_pairs={{0,9},{1,8},{2,11},{3,10},{4,13},{5,12},{6,15},{7,14},{8,1},{9,0},... | collective-permute-start | bytes 405512 | tf_op jit(solution)/shard_map/ppermute | solution.py:336
  34.5 0.0 collective-permute-done.2.rest_2_
  34.5 2.3 %collective-permute-start.6 = (bf16[33,16,128]{2,1,0:T(8,128)(2,1)}, bf16[33,16,128]{2,1,0:T(8,128)(2,1)S(1)}, u32[]{:S(2)}, u32[]{:S(2)}) collective-permute-start(bf16[33,16,128]{2,1,0:T(8,128)(2,1)} %get-tuple-element.31), channel_id=1, source_target_pairs={{0,10},{1,11},{2,8},{3,9},{4,14},{5,15},{6,12},{7,13},{8,2},{9,3},... | collective-permute-start | bytes 405512 | tf_op jit(solution)/shard_map/ppermute | solution.py:336
  36.8 0.0 collective-permute-done.3.rest_3_
  36.8 1.3 %collective-permute-start.7 = (bf16[33,16,128]{2,1,0:T(8,128)(2,1)}, bf16[33,16,128]{2,1,0:T(8,128)(2,1)S(1)}, u32[]{:S(2)}, u32[]{:S(2)}) collective-permute-start(bf16[33,16,128]{2,1,0:T(8,128)(2,1)} %get-tuple-element.32), channel_id=1, source_target_pairs={{0,11},{1,10},{2,9},{3,8},{4,15},{5,14},{6,13},{7,12},{8,3},{9,2},... | collective-permute-start | bytes 405512 | tf_op jit(solution)/shard_map/ppermute | solution.py:336
  38.1 4.1 %collective-permute-done.4.rest_4_ = bf16[33,16,128]{2,1,0:T(8,128)(2,1)S(1)} collective-permute-done((bf16[33,16,128]{2,1,0:T(8,128)(2,1)}, bf16[33,16,128]{2,1,0:T(8,128)(2,1)S(1)}, u32[]{:S(2)}, u32[]{:S(2)}) %collective-permute-start.4) | collective-permute-done | bytes 135200 | tf_op jit(solution)/shard_map/ppermute | solution.py:336
  42.2 1.3 %collective-permute-start.9 = (bf16[65,16,128]{2,1,0:T(8,128)(2,1)}, bf16[65,16,128]{2,1,0:T(8,128)(2,1)S(1)}, u32[]{:S(2)}, u32[]{:S(2)}) collective-permute-start(bf16[65,16,128]{2,1,0:T(8,128)(2,1)} %get-tuple-element.34), channel_id=1, source_target_pairs={{0,12},{1,13},{2,14},{3,15},{4,8},{5,9},{6,10},{7,11},{8,4},{9,5},... | collective-permute-start | bytes 798728 | tf_op jit(solution)/shard_map/ppermute | solution.py:336
  43.5 4.0 %collective-permute-done.5.rest_5_ = bf16[33,16,128]{2,1,0:T(8,128)(2,1)S(1)} collective-permute-done((bf16[33,16,128]{2,1,0:T(8,128)(2,1)}, bf16[33,16,128]{2,1,0:T(8,128)(2,1)S(1)}, u32[]{:S(2)}, u32[]{:S(2)}) %collective-permute-start.5) | collective-permute-done | bytes 135200 | tf_op jit(solution)/shard_map/ppermute | solution.py:336
  47.5 11.7 %collective-permute-start.10 = (bf16[65,16,128]{2,1,0:T(8,128)(2,1)}, bf16[65,16,128]{2,1,0:T(8,128)(2,1)S(1)}, u32[]{:S(2)}, u32[]{:S(2)}) collective-permute-start(bf16[65,16,128]{2,1,0:T(8,128)(2,1)} %get-tuple-element.35), channel_id=1, source_target_pairs={{0,3},{1,2},{2,1},{3,0},{4,7},{5,6},{6,5},{7,4},{8,11},{9,10},{10,... | collective-permute-start | bytes 798728 | tf_op jit(solution)/shard_map/ppermute | solution.py:336
  59.2 0.0 collective-permute-done.6.rest_6_
  59.2 3.6 %collective-permute-start.11 = (bf16[65,16,128]{2,1,0:T(8,128)(2,1)}, bf16[65,16,128]{2,1,0:T(8,128)(2,1)S(1)}, u32[]{:S(2)}, u32[]{:S(2)}) collective-permute-start(bf16[65,16,128]{2,1,0:T(8,128)(2,1)} %get-tuple-element.36), channel_id=1, source_target_pairs={{0,5},{1,4},{2,7},{3,6},{4,1},{5,0},{6,3},{7,2},{8,13},{9,12},{10,... | collective-permute-start | bytes 798728 | tf_op jit(solution)/shard_map/ppermute | solution.py:336
  62.8 0.0 collective-permute-done.7.rest_7_
  62.8 1.1 collective-permute-start.12
  64.0 0.0 collective-permute-done.8.rest_8_
  64.0 0.2 collective-permute-start.13
  64.2 0.7 reshape.9.correction_ref
  64.9 10.8 %collective-permute-done.9.rest_9_ = bf16[65,16,128]{2,1,0:T(8,128)(2,1)S(1)} collective-permute-done((bf16[65,16,128]{2,1,0:T(8,128)(2,1)}, bf16[65,16,128]{2,1,0:T(8,128)(2,1)S(1)}, u32[]{:S(2)}, u32[]{:S(2)}) %collective-permute-start.9) | collective-permute-done | bytes 266272 | tf_op jit(solution)/shard_map/ppermute | solution.py:336
  75.7 0.0 collective-permute-start.14
  75.7 0.0 collective-permute-done.10.rest_10_
  75.7 0.1 collective-permute-start.15
  75.8 0.0 collective-permute-done.11.rest_11_
  75.8 6.2 %collective-permute-start.16 = (bf16[65,16,128]{2,1,0:T(8,128)(2,1)}, bf16[65,16,128]{2,1,0:T(8,128)(2,1)S(1)}, u32[]{:S(2)}, u32[]{:S(2)}) collective-permute-start(bf16[65,16,128]{2,1,0:T(8,128)(2,1)} %get-tuple-element.41), channel_id=1, source_target_pairs={{0,7},{1,6},{2,5},{3,4},{4,3},{5,2},{6,1},{7,0},{8,15},{9,14},{10,... | collective-permute-start | bytes 798728 | tf_op jit(solution)/shard_map/ppermute | solution.py:336
  82.1 0.0 collective-permute-done.12.rest_12_
  82.1 0.0 collective-permute-start.17
  82.1 0.0 collective-permute-done.13.rest_13_
  82.1 3.8 %collective-permute-start.18 = (bf16[65,16,128]{2,1,0:T(8,128)(2,1)}, bf16[65,16,128]{2,1,0:T(8,128)(2,1)S(1)}, u32[]{:S(2)}, u32[]{:S(2)}) collective-permute-start(bf16[65,16,128]{2,1,0:T(8,128)(2,1)} %get-tuple-element.43), channel_id=1, source_target_pairs={{0,1},{1,0},{2,3},{3,2},{4,5},{5,4},{6,7},{7,6},{8,9},{9,8},{10,11... | collective-permute-start | bytes 798728 | tf_op jit(solution)/shard_map/ppermute | solution.py:336
  85.9 5.7 %scale.1.scaled_hbm = bf16[64,128,256]{2,1,0:T(8,128)(2,1)} custom-call(f32[64,64]{1,0:T(8,128)} %reshape.9.correction_ref, f32[64,128,128]{2,1,0:T(8,128)} %constant.11.clone.table_ref), custom_call_target="tpu_custom_call" | custom-call | flops 6000000000 | bytes 16777216 | tf_op jit(solution)/shard_map/scale/pallas_call | solution.py:233
  91.6 0.0 copy-done.17
  91.7 0.0 collective-permute-done.14.rest_14_
  91.7 0.0 copy-start.7
  91.8 0.5 collective-permute-done.15.rest_15_
  92.2 6.9 %collective-permute-done.16.rest_16_ = bf16[65,16,128]{2,1,0:T(8,128)(2,1)S(1)} collective-permute-done((bf16[65,16,128]{2,1,0:T(8,128)(2,1)}, bf16[65,16,128]{2,1,0:T(8,128)(2,1)S(1)}, u32[]{:S(2)}, u32[]{:S(2)}) %collective-permute-start.16) | collective-permute-done | bytes 266272 | tf_op jit(solution)/shard_map/ppermute | solution.py:336
  99.1 6.4 %collective-permute-done.17.rest_17_ = bf16[65,16,128]{2,1,0:T(8,128)(2,1)S(1)} collective-permute-done((bf16[65,16,128]{2,1,0:T(8,128)(2,1)}, bf16[65,16,128]{2,1,0:T(8,128)(2,1)S(1)}, u32[]{:S(2)}, u32[]{:S(2)}) %collective-permute-start.17) | collective-permute-done | bytes 266272 | tf_op jit(solution)/shard_map/ppermute | solution.py:336
  105.5 0.0 collective-permute-done.18.rest_18_
  105.6 0.7 copy-done.10
  106.2 0.1 copy-done.11
  106.3 9.9 %final.1 = f32[2,2,64,64,128]{4,3,2,1,0:T(8,128)} custom-call(bf16[64,128,256]{2,1,0:T(8,128)(2,1)} %scale.1.scaled_hbm, bf16[32,16,128]{2,1,0:T(8,128)(2,1)} %copy-done.16, bf16[32,16,128]{2,1,0:T(8,128)(2,1)} %copy-done.17, bf16[32,16,128]{2,1,0:T(8,128)(2,1)} %copy-done.18, bf16[32,16,128]{2,1,0:T(8,128)(2,1)} %copy-done.19, ...), custom_call_target="tpu_custom_call" | custom-call | flops 8000000000 | bytes 16777216 | tf_op jit(solution)/shard_map/final/pallas_call | solution.py:311
  (36 shorter events, 0.1 us)
Async XLA Ops:
  7.6 23.9 %collective-permute-start = (bf16[32,16,128]{2,1,0:T(8,128)(2,1)}, bf16[32,16,128]{2,1,0:T(8,128)(2,1)S(1)}, u32[]{:S(2)}, u32[]{:S(2)}) collective-permute-start(bf16[32,16,128]{2,1,0:T(8,128)(2,1)} %get-tuple-element.25), channel_id=1, source_target_pairs={{0,8},{1,9},{2,10},{3,11},{4,12},{5,13},{6,14},{7,15},{8,0},{9,1},... | collective-permute-start | bytes 393224 | tf_op jit(solution)/shard_map/ppermute | solution.py:336
  10.0 23.3 %collective-permute-start.1 = (bf16[32,16,128]{2,1,0:T(8,128)(2,1)}, bf16[32,16,128]{2,1,0:T(8,128)(2,1)S(1)}, u32[]{:S(2)}, u32[]{:S(2)}) collective-permute-start(bf16[32,16,128]{2,1,0:T(8,128)(2,1)} %get-tuple-element.26), channel_id=1, source_target_pairs={{0,9},{1,8},{2,11},{3,10},{4,13},{5,12},{6,15},{7,14},{8,1},{9,0},... | collective-permute-start | bytes 393224 | tf_op jit(solution)/shard_map/ppermute | solution.py:336
  10.9 23.6 %collective-permute-start.2 = (bf16[32,16,128]{2,1,0:T(8,128)(2,1)}, bf16[32,16,128]{2,1,0:T(8,128)(2,1)S(1)}, u32[]{:S(2)}, u32[]{:S(2)}) collective-permute-start(bf16[32,16,128]{2,1,0:T(8,128)(2,1)} %get-tuple-element.27), channel_id=1, source_target_pairs={{0,10},{1,11},{2,8},{3,9},{4,14},{5,15},{6,12},{7,13},{8,2},{9,3},... | collective-permute-start | bytes 393224 | tf_op jit(solution)/shard_map/ppermute | solution.py:336
  13.1 23.6 %collective-permute-start.3 = (bf16[32,16,128]{2,1,0:T(8,128)(2,1)}, bf16[32,16,128]{2,1,0:T(8,128)(2,1)S(1)}, u32[]{:S(2)}, u32[]{:S(2)}) collective-permute-start(bf16[32,16,128]{2,1,0:T(8,128)(2,1)} %get-tuple-element.28), channel_id=1, source_target_pairs={{0,11},{1,10},{2,9},{3,8},{4,15},{5,14},{6,13},{7,12},{8,3},{9,2},... | collective-permute-start | bytes 393224 | tf_op jit(solution)/shard_map/ppermute | solution.py:336
  16.9 47.3 %copy-start = (f32[4096]{0:T(1024)S(1)}, f32[4096]{0:T(1024)}, u32[]{:S(2)}) copy-start(f32[4096]{0:T(1024)} %param.15) | copy-start | bytes 49156
  31.3 32.7 %collective-permute-start.8 = (bf16[65,16,128]{2,1,0:T(8,128)(2,1)}, bf16[65,16,128]{2,1,0:T(8,128)(2,1)S(1)}, u32[]{:S(2)}, u32[]{:S(2)}) collective-permute-start(bf16[65,16,128]{2,1,0:T(8,128)(2,1)} %get-tuple-element.33), channel_id=1, source_target_pairs={{0,4},{1,5},{2,6},{3,7},{4,0},{5,1},{6,2},{7,3},{8,12},{9,13},{10,... | collective-permute-start | bytes 798728 | tf_op jit(solution)/shard_map/ppermute | solution.py:336
  31.5 60.1 %copy-start.16 = (bf16[32,16,128]{2,1,0:T(8,128)(2,1)}, bf16[32,16,128]{2,1,0:T(8,128)(2,1)S(1)}, u32[]{:S(2)}) copy-start(bf16[32,16,128]{2,1,0:T(8,128)(2,1)S(1)} %collective-permute-done.rest_0_) | copy-start | bytes 393220
  31.5 10.7 %collective-permute-start.4 = (bf16[33,16,128]{2,1,0:T(8,128)(2,1)}, bf16[33,16,128]{2,1,0:T(8,128)(2,1)S(1)}, u32[]{:S(2)}, u32[]{:S(2)}) collective-permute-start(bf16[33,16,128]{2,1,0:T(8,128)(2,1)} %get-tuple-element.29), channel_id=1, source_target_pairs={{0,8},{1,9},{2,10},{3,11},{4,12},{5,13},{6,14},{7,15},{8,0},{9,1},... | collective-permute-start | bytes 405512 | tf_op jit(solution)/shard_map/ppermute | solution.py:336
  33.3 58.3 %copy-start.17 = (bf16[32,16,128]{2,1,0:T(8,128)(2,1)}, bf16[32,16,128]{2,1,0:T(8,128)(2,1)S(1)}, u32[]{:S(2)}) copy-start(bf16[32,16,128]{2,1,0:T(8,128)(2,1)S(1)} %collective-permute-done.1.rest_1_) | copy-start | bytes 393220
  33.3 14.1 %collective-permute-start.5 = (bf16[33,16,128]{2,1,0:T(8,128)(2,1)}, bf16[33,16,128]{2,1,0:T(8,128)(2,1)S(1)}, u32[]{:S(2)}, u32[]{:S(2)}) collective-permute-start(bf16[33,16,128]{2,1,0:T(8,128)(2,1)} %get-tuple-element.30), channel_id=1, source_target_pairs={{0,9},{1,8},{2,11},{3,10},{4,13},{5,12},{6,15},{7,14},{8,1},{9,0},... | collective-permute-start | bytes 405512 | tf_op jit(solution)/shard_map/ppermute | solution.py:336
  34.5 57.1 %copy-start.18 = (bf16[32,16,128]{2,1,0:T(8,128)(2,1)}, bf16[32,16,128]{2,1,0:T(8,128)(2,1)S(1)}, u32[]{:S(2)}) copy-start(bf16[32,16,128]{2,1,0:T(8,128)(2,1)S(1)} %collective-permute-done.2.rest_2_) | copy-start | bytes 393220
  34.5 24.7 %collective-permute-start.6 = (bf16[33,16,128]{2,1,0:T(8,128)(2,1)}, bf16[33,16,128]{2,1,0:T(8,128)(2,1)S(1)}, u32[]{:S(2)}, u32[]{:S(2)}) collective-permute-start(bf16[33,16,128]{2,1,0:T(8,128)(2,1)} %get-tuple-element.31), channel_id=1, source_target_pairs={{0,10},{1,11},{2,8},{3,9},{4,14},{5,15},{6,12},{7,13},{8,2},{9,3},... | collective-permute-start | bytes 405512 | tf_op jit(solution)/shard_map/ppermute | solution.py:336
  36.8 54.9 %copy-start.19 = (bf16[32,16,128]{2,1,0:T(8,128)(2,1)}, bf16[32,16,128]{2,1,0:T(8,128)(2,1)S(1)}, u32[]{:S(2)}) copy-start(bf16[32,16,128]{2,1,0:T(8,128)(2,1)S(1)} %collective-permute-done.3.rest_3_) | copy-start | bytes 393220
  36.8 26.1 %collective-permute-start.7 = (bf16[33,16,128]{2,1,0:T(8,128)(2,1)}, bf16[33,16,128]{2,1,0:T(8,128)(2,1)S(1)}, u32[]{:S(2)}, u32[]{:S(2)}) collective-permute-start(bf16[33,16,128]{2,1,0:T(8,128)(2,1)} %get-tuple-element.32), channel_id=1, source_target_pairs={{0,11},{1,10},{2,9},{3,8},{4,15},{5,14},{6,13},{7,12},{8,3},{9,2},... | collective-permute-start | bytes 405512 | tf_op jit(solution)/shard_map/ppermute | solution.py:336
  42.2 49.4 %copy-start.12 = (bf16[33,16,128]{2,1,0:T(8,128)(2,1)}, bf16[33,16,128]{2,1,0:T(8,128)(2,1)S(1)}, u32[]{:S(2)}) copy-start(bf16[33,16,128]{2,1,0:T(8,128)(2,1)S(1)} %collective-permute-done.4.rest_4_) | copy-start | bytes 405508
  42.2 33.5 %collective-permute-start.9 = (bf16[65,16,128]{2,1,0:T(8,128)(2,1)}, bf16[65,16,128]{2,1,0:T(8,128)(2,1)S(1)}, u32[]{:S(2)}, u32[]{:S(2)}) collective-permute-start(bf16[65,16,128]{2,1,0:T(8,128)(2,1)} %get-tuple-element.34), channel_id=1, source_target_pairs={{0,12},{1,13},{2,14},{3,15},{4,8},{5,9},{6,10},{7,11},{8,4},{9,5},... | collective-permute-start | bytes 798728 | tf_op jit(solution)/shard_map/ppermute | solution.py:336
  47.5 44.2 %copy-start.13 = (bf16[33,16,128]{2,1,0:T(8,128)(2,1)}, bf16[33,16,128]{2,1,0:T(8,128)(2,1)S(1)}, u32[]{:S(2)}) copy-start(bf16[33,16,128]{2,1,0:T(8,128)(2,1)S(1)} %collective-permute-done.5.rest_5_) | copy-start | bytes 405508
  47.5 28.3 %collective-permute-start.10 = (bf16[65,16,128]{2,1,0:T(8,128)(2,1)}, bf16[65,16,128]{2,1,0:T(8,128)(2,1)S(1)}, u32[]{:S(2)}, u32[]{:S(2)}) collective-permute-start(bf16[65,16,128]{2,1,0:T(8,128)(2,1)} %get-tuple-element.35), channel_id=1, source_target_pairs={{0,3},{1,2},{2,1},{3,0},{4,7},{5,6},{6,5},{7,4},{8,11},{9,10},{10,... | collective-permute-start | bytes 798728 | tf_op jit(solution)/shard_map/ppermute | solution.py:336
  59.2 32.4 %copy-start.14 = (bf16[33,16,128]{2,1,0:T(8,128)(2,1)}, bf16[33,16,128]{2,1,0:T(8,128)(2,1)S(1)}, u32[]{:S(2)}) copy-start(bf16[33,16,128]{2,1,0:T(8,128)(2,1)S(1)} %collective-permute-done.6.rest_6_) | copy-start | bytes 405508
  59.2 16.6 %collective-permute-start.11 = (bf16[65,16,128]{2,1,0:T(8,128)(2,1)}, bf16[65,16,128]{2,1,0:T(8,128)(2,1)S(1)}, u32[]{:S(2)}, u32[]{:S(2)}) collective-permute-start(bf16[65,16,128]{2,1,0:T(8,128)(2,1)} %get-tuple-element.36), channel_id=1, source_target_pairs={{0,5},{1,4},{2,7},{3,6},{4,1},{5,0},{6,3},{7,2},{8,13},{9,12},{10,... | collective-permute-start | bytes 798728 | tf_op jit(solution)/shard_map/ppermute | solution.py:336
  62.8 28.8 %copy-start.15 = (bf16[33,16,128]{2,1,0:T(8,128)(2,1)}, bf16[33,16,128]{2,1,0:T(8,128)(2,1)S(1)}, u32[]{:S(2)}) copy-start(bf16[33,16,128]{2,1,0:T(8,128)(2,1)S(1)} %collective-permute-done.7.rest_7_) | copy-start | bytes 405508
  62.8 19.2 %collective-permute-start.12 = (bf16[65,16,128]{2,1,0:T(8,128)(2,1)}, bf16[65,16,128]{2,1,0:T(8,128)(2,1)S(1)}, u32[]{:S(2)}, u32[]{:S(2)}) collective-permute-start(bf16[65,16,128]{2,1,0:T(8,128)(2,1)} %get-tuple-element.37), channel_id=1, source_target_pairs={{0,13},{1,12},{2,15},{3,14},{4,9},{5,8},{6,11},{7,10},{8,5},{9,4},... | collective-permute-start | bytes 798728 | tf_op jit(solution)/shard_map/ppermute | solution.py:336
  64.0 27.7 %copy-start.1 = (bf16[65,16,128]{2,1,0:T(8,128)(2,1)}, bf16[65,16,128]{2,1,0:T(8,128)(2,1)S(1)}, u32[]{:S(2)}) copy-start(bf16[65,16,128]{2,1,0:T(8,128)(2,1)S(1)} %collective-permute-done.8.rest_8_) | copy-start | bytes 798724
  64.0 18.1 %collective-permute-start.13 = (bf16[65,16,128]{2,1,0:T(8,128)(2,1)}, bf16[65,16,128]{2,1,0:T(8,128)(2,1)S(1)}, u32[]{:S(2)}, u32[]{:S(2)}) collective-permute-start(bf16[65,16,128]{2,1,0:T(8,128)(2,1)} %get-tuple-element.38), channel_id=1, source_target_pairs={{0,2},{1,3},{2,0},{3,1},{4,6},{5,7},{6,4},{7,5},{8,10},{9,11},{10,... | collective-permute-start | bytes 798728 | tf_op jit(solution)/shard_map/ppermute | solution.py:336
  75.7 16.0 %copy-start.2 = (bf16[65,16,128]{2,1,0:T(8,128)(2,1)}, bf16[65,16,128]{2,1,0:T(8,128)(2,1)S(1)}, u32[]{:S(2)}) copy-start(bf16[65,16,128]{2,1,0:T(8,128)(2,1)S(1)} %collective-permute-done.9.rest_9_) | copy-start | bytes 798724
  75.7 16.0 %collective-permute-start.14 = (bf16[65,16,128]{2,1,0:T(8,128)(2,1)}, bf16[65,16,128]{2,1,0:T(8,128)(2,1)S(1)}, u32[]{:S(2)}, u32[]{:S(2)}) collective-permute-start(bf16[65,16,128]{2,1,0:T(8,128)(2,1)} %get-tuple-element.39), channel_id=1, source_target_pairs={{0,6},{1,7},{2,4},{3,5},{4,2},{5,3},{6,0},{7,1},{8,14},{9,15},{10,... | collective-permute-start | bytes 798728 | tf_op jit(solution)/shard_map/ppermute | solution.py:336
  75.7 16.0 %copy-start.3 = (bf16[65,16,128]{2,1,0:T(8,128)(2,1)}, bf16[65,16,128]{2,1,0:T(8,128)(2,1)S(1)}, u32[]{:S(2)}) copy-start(bf16[65,16,128]{2,1,0:T(8,128)(2,1)S(1)} %collective-permute-done.10.rest_10_) | copy-start | bytes 798724
  75.7 16.5 %collective-permute-start.15 = (bf16[65,16,128]{2,1,0:T(8,128)(2,1)}, bf16[65,16,128]{2,1,0:T(8,128)(2,1)S(1)}, u32[]{:S(2)}, u32[]{:S(2)}) collective-permute-start(bf16[65,16,128]{2,1,0:T(8,128)(2,1)} %get-tuple-element.40), channel_id=1, source_target_pairs={{0,14},{1,15},{2,12},{3,13},{4,10},{5,11},{6,8},{7,9},{8,6},{9,7},... | collective-permute-start | bytes 798728 | tf_op jit(solution)/shard_map/ppermute | solution.py:336
  75.8 15.9 %copy-start.4 = (bf16[65,16,128]{2,1,0:T(8,128)(2,1)}, bf16[65,16,128]{2,1,0:T(8,128)(2,1)S(1)}, u32[]{:S(2)}) copy-start(bf16[65,16,128]{2,1,0:T(8,128)(2,1)S(1)} %collective-permute-done.11.rest_11_) | copy-start | bytes 798724
  75.8 23.3 %collective-permute-start.16 = (bf16[65,16,128]{2,1,0:T(8,128)(2,1)}, bf16[65,16,128]{2,1,0:T(8,128)(2,1)S(1)}, u32[]{:S(2)}, u32[]{:S(2)}) collective-permute-start(bf16[65,16,128]{2,1,0:T(8,128)(2,1)} %get-tuple-element.41), channel_id=1, source_target_pairs={{0,7},{1,6},{2,5},{3,4},{4,3},{5,2},{6,1},{7,0},{8,15},{9,14},{10,... | collective-permute-start | bytes 798728 | tf_op jit(solution)/shard_map/ppermute | solution.py:336
  82.1 9.6 %copy-start.5 = (bf16[65,16,128]{2,1,0:T(8,128)(2,1)}, bf16[65,16,128]{2,1,0:T(8,128)(2,1)S(1)}, u32[]{:S(2)}) copy-start(bf16[65,16,128]{2,1,0:T(8,128)(2,1)S(1)} %collective-permute-done.12.rest_12_) | copy-start | bytes 798724
  82.1 23.5 %collective-permute-start.17 = (bf16[65,16,128]{2,1,0:T(8,128)(2,1)}, bf16[65,16,128]{2,1,0:T(8,128)(2,1)S(1)}, u32[]{:S(2)}, u32[]{:S(2)}) collective-permute-start(bf16[65,16,128]{2,1,0:T(8,128)(2,1)} %get-tuple-element.42), channel_id=1, source_target_pairs={{0,15},{1,14},{2,13},{3,12},{4,11},{5,10},{6,9},{7,8},{8,7},{9,6},... | collective-permute-start | bytes 798728 | tf_op jit(solution)/shard_map/ppermute | solution.py:336
  82.1 9.6 %copy-start.6 = (bf16[65,16,128]{2,1,0:T(8,128)(2,1)}, bf16[65,16,128]{2,1,0:T(8,128)(2,1)S(1)}, u32[]{:S(2)}) copy-start(bf16[65,16,128]{2,1,0:T(8,128)(2,1)S(1)} %collective-permute-done.13.rest_13_) | copy-start | bytes 798724
  82.1 23.4 %collective-permute-start.18 = (bf16[65,16,128]{2,1,0:T(8,128)(2,1)}, bf16[65,16,128]{2,1,0:T(8,128)(2,1)S(1)}, u32[]{:S(2)}, u32[]{:S(2)}) collective-permute-start(bf16[65,16,128]{2,1,0:T(8,128)(2,1)} %get-tuple-element.43), channel_id=1, source_target_pairs={{0,1},{1,0},{2,3},{3,2},{4,5},{5,4},{6,7},{7,6},{8,9},{9,8},{10,11... | collective-permute-start | bytes 798728 | tf_op jit(solution)/shard_map/ppermute | solution.py:336
  91.7 13.8 %copy-start.7 = (bf16[65,16,128]{2,1,0:T(8,128)(2,1)}, bf16[65,16,128]{2,1,0:T(8,128)(2,1)S(1)}, u32[]{:S(2)}) copy-start(bf16[65,16,128]{2,1,0:T(8,128)(2,1)S(1)} %collective-permute-done.14.rest_14_) | copy-start | bytes 798724
  92.2 13.3 %copy-start.8 = (bf16[65,16,128]{2,1,0:T(8,128)(2,1)}, bf16[65,16,128]{2,1,0:T(8,128)(2,1)S(1)}, u32[]{:S(2)}) copy-start(bf16[65,16,128]{2,1,0:T(8,128)(2,1)S(1)} %collective-permute-done.15.rest_15_) | copy-start | bytes 798724
  99.1 6.4 %copy-start.9 = (bf16[65,16,128]{2,1,0:T(8,128)(2,1)}, bf16[65,16,128]{2,1,0:T(8,128)(2,1)S(1)}, u32[]{:S(2)}) copy-start(bf16[65,16,128]{2,1,0:T(8,128)(2,1)S(1)} %collective-permute-done.16.rest_16_) | copy-start | bytes 798724
  105.5 0.7 copy-start.10
  105.5 0.8 copy-start.11
